TPU v7x, 128 devices: a whole 4x4x4 slice. The times are simulated.
128 devices in a mesh: dp: 8 (over y, core), tm: 16 (over z, x).
Axes of the slice: x: 4, y: 4, z: 4, core: 2. Of those that a mesh axis runs over, the one named last changes fastest.
Arguments:
- tokens: bfloat16 [8, 16, 384, 2048], P('dp', 'tm'), may hold values from -6 to 6
- cotangent: bfloat16 [8, 16, 384, 2048], P('dp', 'tm'), may hold values from -6 to 6
- norm_gain: bfloat16 [2048], replicated, may hold values from 0.25 to 1.75
- w_query: bfloat16 [2048, 1024], P(('dp', 'tm'))
- w_key: bfloat16 [2048, 1024], P(('dp', 'tm'))
- w_value: bfloat16 [2048, 1024], P(('dp', 'tm')), may hold values from -0.125 to 0.125
- w_out: bfloat16 [1024, 2048], P(('dp', 'tm')), may hold values from -0.1875 to 0.1875
Outputs:
- mixed: bfloat16 [8, 16, 384, 2048], P('dp', 'tm')
- grad_tokens: bfloat16 [8, 16, 384, 2048], P('dp', 'tm')
- grad_gain: float32 [2048], P(('dp', 'tm'))
- grad_query: float32 [2048, 1024], P(('dp', 'tm'))
- grad_key: float32 [2048, 1024], P(('dp', 'tm'))
- grad_value: float32 [2048, 1024], P(('dp', 'tm'))
- grad_out: float32 [1024, 2048], P(('dp', 'tm'))
All inputs are finite; a program needn't handle non-finite values.
Results may differ from a plain program's by a relative error of at most 0.024.
The roundings to bfloat16 on the way count: a program that leaves them out, or rounds other values in their place, can miss the bound.
Values may be sent and summed in bfloat16 or wider, within the bound.
A program may use at most 128 MiB of HBM per device.

v0:
```python
import jax
import jax.numpy as jnp
from jax import lax
from jax.sharding import PartitionSpec as P

HEADS = 8
HEAD = 128


def split_heads(array):
    return array.reshape(array.shape[:3] + (HEADS, HEAD))


def attend(query, keys, values, upstream):
    shape = query.shape
    factor = HEAD ** (-0.5)
    q_heads = split_heads(query)
    k_heads = split_heads(keys)
    v_heads = split_heads(values)
    d_heads = split_heads(upstream)
    scores = (
        jnp.einsum("cfphe,cgphe->cphfg", q_heads, k_heads, preferred_element_type=jnp.float32)
        * factor
    )
    later = lax.broadcasted_iota(jnp.int32, (shape[1], shape[1]), 0)
    earlier = lax.broadcasted_iota(jnp.int32, (shape[1], shape[1]), 1)
    scores = jnp.where(earlier <= later, scores, -1e30)
    highest = jnp.max(scores, axis=-1, keepdims=True)
    weights = jnp.exp(scores - highest)
    prob = weights / jnp.sum(weights, axis=-1, keepdims=True)
    prob_b = prob.astype(jnp.bfloat16)
    attended = (
        jnp.einsum("cphfg,cgphe->cfphe", prob_b, v_heads, preferred_element_type=jnp.float32)
        .astype(jnp.bfloat16)
        .reshape(shape)
    )
    dprob = jnp.einsum("cfphe,cgphe->cphfg", d_heads, v_heads, preferred_element_type=jnp.float32)
    dscore = prob * (dprob - jnp.sum(prob * dprob, axis=-1, keepdims=True))
    dscore_b = dscore.astype(jnp.bfloat16)
    dquery = (
        (
            jnp.einsum("cphfg,cgphe->cfphe", dscore_b, k_heads, preferred_element_type=jnp.float32)
            * factor
        )
        .astype(jnp.bfloat16)
        .reshape(shape)
    )
    dkeys = (
        (
            jnp.einsum("cphfg,cfphe->cgphe", dscore_b, q_heads, preferred_element_type=jnp.float32)
            * factor
        )
        .astype(jnp.bfloat16)
        .reshape(shape)
    )
    dvalues = (
        jnp.einsum("cphfg,cfphe->cgphe", prob_b, d_heads, preferred_element_type=jnp.float32)
        .astype(jnp.bfloat16)
        .reshape(shape)
    )
    return (attended, dquery, dkeys, dvalues)


def transpose_dot(left, right):
    return lax.dot_general(
        left, right, (((0,), (0,)), ((), ())), preferred_element_type=jnp.float32
    )


def on_device(tokens, cotangent, norm_gain, w_query, w_key, w_value, w_out):
    full_query, full_key, full_value, full_out = (
        lax.all_gather(w_query, ("dp", "tm"), axis=0, tiled=True),
        lax.all_gather(w_key, ("dp", "tm"), axis=0, tiled=True),
        lax.all_gather(w_value, ("dp", "tm"), axis=0, tiled=True),
        lax.all_gather(w_out, ("dp", "tm"), axis=0, tiled=True),
    )
    values_in = tokens[0, 0].astype(jnp.float32)
    upstream_rows = cotangent[0, 0]
    gain = norm_gain.astype(jnp.float32)
    centre = jnp.mean(values_in, axis=-1, keepdims=True)
    centered = values_in - centre
    variance = jnp.mean(centered * centered, axis=-1, keepdims=True)
    inverse = lax.rsqrt(variance + 1e-05)
    scaled = centered * inverse
    normed = (scaled * gain).astype(jnp.bfloat16)
    query = jnp.dot(normed, full_query, preferred_element_type=jnp.float32).astype(jnp.bfloat16)
    keys = jnp.dot(normed, full_key, preferred_element_type=jnp.float32).astype(jnp.bfloat16)
    values = jnp.dot(normed, full_value, preferred_element_type=jnp.float32).astype(jnp.bfloat16)
    upstream = lax.dot_general(
        upstream_rows, full_out, (((1,), (1,)), ((), ())), preferred_element_type=jnp.float32
    ).astype(jnp.bfloat16)
    t_query, t_keys, t_values, t_upstream = (
        lax.all_to_all(query[None], "tm", split_axis=1, concat_axis=0, tiled=True),
        lax.all_to_all(keys[None], "tm", split_axis=1, concat_axis=0, tiled=True),
        lax.all_to_all(values[None], "tm", split_axis=1, concat_axis=0, tiled=True),
        lax.all_to_all(upstream[None], "tm", split_axis=1, concat_axis=0, tiled=True),
    )
    attended, dquery, dkeys, dvalues = attend(
        t_query[None], t_keys[None], t_values[None], t_upstream[None]
    )
    back_att, back_dq, back_dk, back_dv = (
        lax.all_to_all(attended[0], "tm", split_axis=0, concat_axis=1, tiled=True),
        lax.all_to_all(dquery[0], "tm", split_axis=0, concat_axis=1, tiled=True),
        lax.all_to_all(dkeys[0], "tm", split_axis=0, concat_axis=1, tiled=True),
        lax.all_to_all(dvalues[0], "tm", split_axis=0, concat_axis=1, tiled=True),
    )
    back_att, back_dq, back_dk, back_dv = (back_att[0], back_dq[0], back_dk[0], back_dv[0])
    mixed = (values_in + jnp.dot(back_att, full_out, preferred_element_type=jnp.float32)).astype(
        jnp.bfloat16
    )
    dnormed = lax.dot_general(
        back_dq, full_query, (((1,), (1,)), ((), ())), preferred_element_type=jnp.float32
    )
    dnormed = dnormed + lax.dot_general(
        back_dk, full_key, (((1,), (1,)), ((), ())), preferred_element_type=jnp.float32
    )
    dnormed = dnormed + lax.dot_general(
        back_dv, full_value, (((1,), (1,)), ((), ())), preferred_element_type=jnp.float32
    )
    dscaled = dnormed * gain
    first_mean = jnp.mean(dscaled, axis=-1, keepdims=True)
    second_mean = jnp.mean(dscaled * scaled, axis=-1, keepdims=True)
    grad_rows = (
        inverse * (dscaled - first_mean - scaled * second_mean) + upstream_rows.astype(jnp.float32)
    ).astype(jnp.bfloat16)
    terms = (
        transpose_dot(normed, back_dq),
        transpose_dot(normed, back_dk),
        transpose_dot(normed, back_dv),
        transpose_dot(back_att, upstream_rows),
        jnp.sum(dnormed * scaled, axis=0),
    )
    partial_sums = (
        lax.psum_scatter(
            terms[0].astype(jnp.bfloat16), "dp", scatter_dimension=0, tiled=True
        ).astype(jnp.float32),
        lax.psum_scatter(
            terms[1].astype(jnp.bfloat16), "dp", scatter_dimension=0, tiled=True
        ).astype(jnp.float32),
        lax.psum_scatter(
            terms[2].astype(jnp.bfloat16), "dp", scatter_dimension=0, tiled=True
        ).astype(jnp.float32),
        lax.psum_scatter(
            terms[3].astype(jnp.bfloat16), "dp", scatter_dimension=0, tiled=True
        ).astype(jnp.float32),
        lax.psum_scatter(
            terms[4].astype(jnp.bfloat16), "dp", scatter_dimension=0, tiled=True
        ).astype(jnp.float32),
    )
    totals = (
        lax.psum_scatter(
            partial_sums[0].astype(jnp.bfloat16), "tm", scatter_dimension=0, tiled=True
        ).astype(jnp.float32),
        lax.psum_scatter(
            partial_sums[1].astype(jnp.bfloat16), "tm", scatter_dimension=0, tiled=True
        ).astype(jnp.float32),
        lax.psum_scatter(
            partial_sums[2].astype(jnp.bfloat16), "tm", scatter_dimension=0, tiled=True
        ).astype(jnp.float32),
        lax.psum_scatter(
            partial_sums[3].astype(jnp.bfloat16), "tm", scatter_dimension=0, tiled=True
        ).astype(jnp.float32),
        lax.psum_scatter(
            partial_sums[4].astype(jnp.bfloat16), "tm", scatter_dimension=0, tiled=True
        ).astype(jnp.float32),
    )
    grad_query, grad_key, grad_value, grad_out, grad_gain = totals
    return (
        mixed[None, None],
        grad_rows[None, None],
        grad_gain,
        grad_query,
        grad_key,
        grad_value,
        grad_out,
    )


def solution(mesh):
    in_specs = (
        P("dp", "tm", None, None),
        P("dp", "tm", None, None),
        P(),
        P(("dp", "tm"), None),
        P(("dp", "tm"), None),
        P(("dp", "tm"), None),
        P(("dp", "tm"), None),
    )
    out_specs = (
        P("dp", "tm", None, None),
        P("dp", "tm", None, None),
        P(("dp", "tm")),
        P(("dp", "tm"), None),
        P(("dp", "tm"), None),
        P(("dp", "tm"), None),
        P(("dp", "tm"), None),
    )
    return jax.shard_map(
        on_device, mesh=mesh, in_specs=in_specs, out_specs=out_specs, check_vma=False
    )
```

profile of v0, /device:TPU:1, one launch (start us, length us, event | category | flops | bytes accessed | tf_op | source)
XLA Modules:
  0.0 804.3 jit_solution(6944288884339867587)
XLA Ops:
  10.7 1.7 convert_reduce_fusion
  12.4 2.0 fusion.16
  14.3 67.4 %all-gather.5.cloned.1.call-done = bf16[2048,1024]{1,0:T(8,128)(2,1)} async-done(((bf16[16,1024]{1,0:T(8,128)(2,1)}), bf16[2048,1024]{1,0:T(8,128)(2,1)}) %all-gather.5.cloned.1.call-update) | async-done | bytes 4194320 | tf_op jit(solution)/shard_map/all_gather | solution.py:74
  81.7 4.0 fusion.32
  85.7 1.2 copy.103
  87.5 6.1 reduce.15
  93.6 3.2 reshape.210
  96.8 4.5 all-to-all-start
  101.3 49.8 %all-gather.9.cloned.1.call-done = bf16[2048,1024]{1,0:T(8,128)(2,1)} async-done(((bf16[16,1024]{1,0:T(8,128)(2,1)}), bf16[2048,1024]{1,0:T(8,128)(2,1)}) %all-gather.9.cloned.1.call-update) | async-done | bytes 4194320 | tf_op jit(solution)/shard_map/all_gather | solution.py:73
  151.1 4.0 fusion.34
  155.2 1.2 copy.101
  156.4 6.1 reduce.16
  162.5 3.2 reshape.212
  165.7 4.7 all-to-all-start.2
  170.4 50.5 %all-gather.7.cloned.1.call-done = bf16[2048,1024]{1,0:T(8,128)(2,1)} async-done(((bf16[16,1024]{1,0:T(8,128)(2,1)}), bf16[2048,1024]{1,0:T(8,128)(2,1)}) %all-gather.7.cloned.1.call-update) | async-done | bytes 4194320 | tf_op jit(solution)/shard_map/all_gather | solution.py:72
  220.9 4.0 fusion.33
  225.0 1.2 copy.102
  226.2 6.1 reduce.17
  232.3 3.2 reshape.214
  235.6 4.3 all-to-all-start.1
  240.1 4.4 reshape.211
  244.5 4.6 bitcast_reduce_fusion.3
  250.1 4.4 reshape.213
  254.5 4.6 bitcast_reduce_fusion.2
  259.1 1.1 copy.70
  260.1 4.6 reshape.215
  264.7 4.6 bitcast_reduce_fusion.1
  269.5 4.1 fusion.59
  273.6 2.1 fusion.35
  276.3 19.7 %all_to_all.32 = bf16[16,24,1024]{2,1,0:T(8,128)(2,1)S(1)} all-to-all(bf16[16,24,1024]{2,1,0:T(8,128)(2,1)S(1)} %squeeze_reshape.12), channel_id=1, replica_groups=mesh['dp'=8,'tm'=16] {'tm'}, dimensions={0} | all-to-all | bytes 1572864 | tf_op jit(solution)/shard_map/all_to_all | solution.py:102
  296.9 5.8 convolution_convert_fusion
  304.1 4.0 fusion.37
  308.1 1.2 copy.100
  309.3 6.1 reduce.18
  315.5 2.5 reshape.216
  318.0 15.7 %all_to_all.33 = bf16[16,2,12288]{2,1,0:T(2,128)(2,1)} all-to-all(bf16[16,2,12288]{2,1,0:T(2,128)(2,1)S(1)} %reshape.216), channel_id=1, replica_groups=mesh['dp'=8,'tm'=16] {'tm'}, dimensions={0} | all-to-all | bytes 1572864 | tf_op jit(solution)/shard_map/all_to_all | solution.py:96
  333.7 4.4 reshape.217
  338.1 4.6 bitcast_reduce_fusion
  342.9 1.2 multiply_reduce_fusion.1
  346.2 1.2 squeeze_reshape.13
  347.4 15.0 %all_to_all.34 = bf16[16,24,1024]{2,1,0:T(8,128)(2,1)S(1)} all-to-all(bf16[16,24,1024]{2,1,0:T(8,128)(2,1)} %squeeze_reshape.13), channel_id=1, replica_groups=mesh['dp'=8,'tm'=16] {'tm'}, dimensions={0} | all-to-all | bytes 1572864 | tf_op jit(solution)/shard_map/all_to_all | solution.py:103
  363.3 4.5 convolution_convert_fusion.3
  370.2 13.9 %all_to_all.35 = bf16[16,24,1024]{2,1,0:T(8,128)(2,1)S(1)} all-to-all(bf16[16,24,1024]{2,1,0:T(8,128)(2,1)S(1)} %squeeze_reshape.14), channel_id=1, replica_groups=mesh['dp'=8,'tm'=16] {'tm'}, dimensions={0} | all-to-all | bytes 1572864 | tf_op jit(solution)/shard_map/all_to_all | solution.py:104
  385.0 4.6 convolution_convert_fusion.2
  389.7 1.4 copy-done.5
  391.0 1.8 fusion.36
  393.4 13.1 %all_to_all.36 = bf16[16,24,1024]{2,1,0:T(8,128)(2,1)S(1)} all-to-all(bf16[16,24,1024]{2,1,0:T(8,128)(2,1)S(1)} %squeeze_reshape.15), channel_id=1, replica_groups=mesh['dp'=8,'tm'=16] {'tm'}, dimensions={0} | all-to-all | bytes 1572864 | tf_op jit(solution)/shard_map/all_to_all | solution.py:105
  406.5 4.5 convolution_convert_fusion.1
  415.6 6.2 fusion.64
  421.7 3.6 fusion.65
  425.3 17.1 %reduce-scatter.12.cloned.1.call-done = bf16[256,1024]{1,0:T(8,128)(2,1)} async-done(((bf16[2048,1024]{1,0:T(8,128)(2,1)}), bf16[256,1024]{1,0:T(8,128)(2,1)}) %reduce-scatter.12.cloned.1.call-update) | async-done | bytes 524304 | tf_op jit(solution)/shard_map/reduce_scatter | solution.py:137
  442.8 8.1 %fusion.15 = (bf16[2048]{0:T(1024)(128)(2,1)S(1)}, f32[384]{0:T(512)S(1)}, f32[384]{0:T(512)S(1)}, f32[384,2048]{1,0:T(8,128)}) fusion(bf16[1,1,384,2048]{3,2,1,0:T(8,128)(2,1)S(1)} %copy-done, f32[384]{0:T(512)S(1)} %add_rsqrt_fusion, f32[384]{0:T(512)S(1)} %broadcast_multiply_fusion.2, f32[2048]{0:T(1024)S(1)} %convert_element_type.129, ...), kind=kOutput, calls=%fused_computation.22 | convolution fusion | flops 1619260672 | bytes 16009216 | tf_op jit(solution)/shard_map/dot_general | solution.py:117
  450.9 15.4 %all-reduce = bf16[2048]{0:T(1024)(128)(2,1)S(1)} all-reduce(bf16[2048]{0:T(1024)(128)(2,1)S(1)} %get-tuple-element.7), channel_id=2, replica_groups=mesh['dp'=8,'tm'=16] {'dp'}, use_global_device_ids=true, to_apply=%region_8.9.clone | all-reduce | flops 2048 | bytes 8192
  466.4 33.6 %all-reduce.1 = bf16[256]{0:T(256)(128)(2,1)S(1)} all-reduce(bf16[256]{0:T(256)(128)(2,1)S(1)} %dynamic-slice.1), channel_id=3, replica_groups=mesh['dp'=8,'tm'=16] {'tm'}, use_global_device_ids=true, to_apply=%region_9.10.clone | all-reduce | flops 256 | bytes 1024
  500.6 5.5 fusion.21
  506.1 4.3 fusion.24
  510.4 60.6 %all-reduce.5.cloned.1.call-done = bf16[128,2048]{1,0:T(8,128)(2,1)} async-done(((bf16[128,2048]{1,0:T(8,128)(2,1)}), bf16[128,2048]{1,0:T(8,128)(2,1)}) %all-reduce.5.cloned.1.call-update) | async-done | bytes 524304
  571.0 1.4 dynamic-slice_convert_fusion
  572.4 73.4 %reduce-scatter.10.cloned.1.call-done = bf16[16,1024]{1,0:T(8,128)(2,1)} async-done(((bf16[256,1024]{1,0:T(8,128)(2,1)}), bf16[16,1024]{1,0:T(8,128)(2,1)}) %reduce-scatter.10.cloned.1.call-update) | async-done | bytes 32784 | tf_op jit(solution)/shard_map/reduce_scatter | solution.py:151
  645.7 1.4 convert_element_type.157
  647.1 73.5 %reduce-scatter.14.cloned.1.call-done = bf16[16,1024]{1,0:T(8,128)(2,1)} async-done(((bf16[256,1024]{1,0:T(8,128)(2,1)}), bf16[16,1024]{1,0:T(8,128)(2,1)}) %reduce-scatter.14.cloned.1.call-update) | async-done | bytes 32784 | tf_op jit(solution)/shard_map/reduce_scatter | solution.py:154
  720.7 1.4 convert_element_type.159
  722.1 73.6 %reduce-scatter.18.cloned.1.call-done = bf16[16,1024]{1,0:T(8,128)(2,1)} async-done(((bf16[256,1024]{1,0:T(8,128)(2,1)}), bf16[16,1024]{1,0:T(8,128)(2,1)}) %reduce-scatter.18.cloned.1.call-update) | async-done | bytes 32784 | tf_op jit(solution)/shard_map/reduce_scatter | solution.py:157
  795.6 1.4 convert_element_type.161
  (91 shorter events, 18.7 us)
Async XLA Ops:
  7.2 74.5 %copy-start = (bf16[1,1,384,2048]{3,2,1,0:T(8,128)(2,1)S(1)}, bf16[1,1,384,2048]{3,2,1,0:T(8,128)(2,1)}, u32[]{:S(2)}) copy-start(bf16[1,1,384,2048]{3,2,1,0:T(8,128)(2,1)} %param.7) | copy-start | bytes 4718596
  7.2 74.5 %all-gather.5.cloned.1.call-start = ((), (), s32[]{:S(2)}) async-start(), calls=%async_computation.15 | async-start | bytes 4227072 | tf_op jit(solution)/shard_map/all_gather | solution.py:74
  7.9 143.2 %all-gather.9.cloned.1.call-start = ((), (), s32[]{:S(2)}) async-start(), calls=%async_computation.17 | async-start | bytes 4227072 | tf_op jit(solution)/shard_map/all_gather | solution.py:73
  8.7 212.3 %all-gather.7.cloned.1.call-start = ((), (), s32[]{:S(2)}) async-start(), calls=%async_computation.16 | async-start | bytes 4227072 | tf_op jit(solution)/shard_map/all_gather | solution.py:72
  9.4 293.8 %all-gather.11.cloned.1.call-start = ((), (), s32[]{:S(2)}) async-start(), calls=%async_computation.18 | async-start | bytes 4227072 | tf_op jit(solution)/shard_map/all_gather | solution.py:75
  96.8 68.9 %all-to-all-start = ((bf16[16,2,12288]{2,1,0:T(2,128)(2,1)}), bf16[16,2,12288]{2,1,0:T(2,128)(2,1)}, u32[]{:S(2)}, u32[]{:S(2)}) async-start(bf16[16,2,12288]{2,1,0:T(2,128)(2,1)} %reshape.210), calls=%async_computation | async-start | bytes 1572864 | tf_op jit(solution)/shard_map/all_to_all | solution.py:95
  165.7 69.8 %all-to-all-start.2 = ((bf16[16,2,12288]{2,1,0:T(2,128)(2,1)}), bf16[16,2,12288]{2,1,0:T(2,128)(2,1)}, u32[]{:S(2)}, u32[]{:S(2)}) async-start(bf16[16,2,12288]{2,1,0:T(2,128)(2,1)} %reshape.212), calls=%async_computation.2 | async-start | bytes 1572864 | tf_op jit(solution)/shard_map/all_to_all | solution.py:94
  235.6 24.6 %all-to-all-start.1 = ((bf16[16,2,12288]{2,1,0:T(2,128)(2,1)}), bf16[16,2,12288]{2,1,0:T(2,128)(2,1)}, u32[]{:S(2)}, u32[]{:S(2)}) async-start(bf16[16,2,12288]{2,1,0:T(2,128)(2,1)} %reshape.214), calls=%async_computation.1 | async-start | bytes 1572864 | tf_op jit(solution)/shard_map/all_to_all | solution.py:93
  239.8 171.3 %reduce-scatter.20.cloned.1.call-start = ((), (), s32[]{:S(2)}) async-start(), calls=%async_computation.25 | async-start | bytes 4718592 | tf_op jit(solution)/shard_map/reduce_scatter | solution.py:143
  269.3 4.3 copy-start.13
  269.5 4.1 copy-start.1
  296.0 0.9 copy-start.8
  302.7 1.4 copy-start.6
  302.7 109.1 %reduce-scatter.8.cloned.1.call-start = ((), (), s32[]{:S(2)}) async-start(), calls=%async_computation.19 | async-start | bytes 4718592 | tf_op jit(solution)/shard_map/reduce_scatter | solution.py:134
  338.1 4.8 copy-start.4
  338.1 4.8 copy-start.14
  342.9 1.3 copy-start.15
  344.1 1.1 copy-start.3
  362.4 0.9 copy-start.9
  367.8 1.1 copy-start.2
  367.9 74.6 %reduce-scatter.12.cloned.1.call-start = ((), (), s32[]{:S(2)}) async-start(), calls=%async_computation.21 | async-start | bytes 4718592 | tf_op jit(solution)/shard_map/reduce_scatter | solution.py:137
  384.1 0.9 copy-start.11
  389.6 1.4 copy-start.5
  389.6 116.4 %reduce-scatter.16.cloned.1.call-start = ((), (), s32[]{:S(2)}) async-start(), calls=%async_computation.23 | async-start | bytes 4718592 | tf_op jit(solution)/shard_map/reduce_scatter | solution.py:140
  411.0 1.4 copy-start.18
  411.0 2.0 copy-start.17
  411.0 4.5 copy-start.10
  411.0 159.9 %all-reduce.5.cloned.1.call-start = ((), (), s32[]{:S(2)}) async-start(), calls=%async_computation.26 | async-start | bytes 1048576
  411.8 234.0 %reduce-scatter.10.cloned.1.call-start = ((), (), s32[]{:S(2)}) async-start(), calls=%async_computation.20 | async-start | bytes 557056 | tf_op jit(solution)/shard_map/reduce_scatter | solution.py:151
  412.4 308.3 %reduce-scatter.14.cloned.1.call-start = ((), (), s32[]{:S(2)}) async-start(), calls=%async_computation.22 | async-start | bytes 557056 | tf_op jit(solution)/shard_map/reduce_scatter | solution.py:154
  415.5 6.2 copy-start.12
  415.6 6.2 copy-start.16
  442.5 353.2 %reduce-scatter.18.cloned.1.call-start = ((), (), s32[]{:S(2)}) async-start(), calls=%async_computation.24 | async-start | bytes 557056 | tf_op jit(solution)/shard_map/reduce_scatter | solution.py:157
  500.6 5.5 copy-start.7
Sparse Core Ops, SparseCore 0:
  11.2 70.5 all-gather.4
  84.8 66.2 all-gather.8
  154.3 66.5 all-gather.6
  223.9 69.0 all-gather.10
  302.8 33.1 reduce-scatter.19
  368.0 35.4 reduce-scatter.7
  405.9 36.5 reduce-scatter.11
  444.9 36.9 reduce-scatter.15
  485.1 85.8 all-reduce.4
  574.3 71.3 reduce-scatter.9
  648.9 71.6 reduce-scatter.13
  724.0 71.5 reduce-scatter.17
where the time goes:
time: 815 us; the launch traced here: 804 us
  waiting for transfers between devices  470 us (58%)
  blocking collectives  126 us (15%)
  matrix products  69.5 us (9%)
  local copies, waits for them, and re-layouts  66.8 us (8%)
  other arithmetic  39.8 us (5%)
  between operations  17 us (2%)
  starting transfers between devices  15 us (2%)
    reduce_scatter x1, waiting for transfers between devices, on_device(): lax.psum_scatter(partial_sums[2].astype(jnp.bfloat16), 'tm', scatter_dime...  73.6 us
    reduce_scatter x1, waiting for transfers between devices, on_device(): lax.psum_scatter(partial_sums[1].astype(jnp.bfloat16), 'tm', scatter_dime...  73.5 us
    reduce_scatter x1, waiting for transfers between devices, on_device(): lax.psum_scatter(partial_sums[0].astype(jnp.bfloat16), 'tm', scatter_dime...  73.4 us
    all_gather x1, waiting for transfers between devices, on_device(): lax.all_gather(w_value, ('dp', 'tm'), axis=0, tiled=True)  67.4 us
    unnamed x13, waiting for transfers between devices  64.4 us
    all_gather x1, waiting for transfers between devices, on_device(): lax.all_gather(w_query, ('dp', 'tm'), axis=0, tiled=True)  50.5 us
    all_gather x1, waiting for transfers between devices, on_device(): lax.all_gather(w_key, ('dp', 'tm'), axis=0, tiled=True)  49.8 us
    unnamed x2, blocking collectives  49 us
  transfers between devices with their start and end apart: 15, of which 8 were waited for; matrix products, arithmetic and copies ran while one was open for 21% of the time, Pallas kernels for 0%

commit v1 on v0

v1 whole, which is shorter than its diff:
```python
import functools

import jax
import jax.numpy as jnp
from jax import lax
from jax.experimental import pallas as pl
from jax.experimental.pallas import tpu as pltpu
from jax.sharding import PartitionSpec as P

MESH = pl.DeviceIdType.MESH
VMEM_LIMIT = 60 * 1024 * 1024


def coords():
    dp, tm = lax.axis_index("dp"), lax.axis_index("tm")
    return lax.div(dp, 2), lax.rem(dp, 2), lax.div(tm, 4), lax.rem(tm, 4)


def device(y, c, z, x):
    return {"dp": y * 2 + c, "tm": z * 4 + x}


def up(p, d):
    return lax.rem(p + d, 4)


def rcopy(src, dst, sems, i, where):
    return pltpu.make_async_remote_copy(
        src_ref=src,
        dst_ref=dst,
        send_sem=sems[0].at[i],
        recv_sem=sems[1].at[i],
        device_id=where,
        device_id_type=MESH,
    )


OFFSETS = [
    (0, 1), (0, 3), (1, 0), (3, 0), (1, 1), (3, 3), (1, 3), (3, 1),
    (2, 2), (0, 2), (2, 0), (2, 1), (2, 3), (1, 2), (3, 2),
]


def greet(y, c, z, x, tm_peers=True):
    barrier = pltpu.get_barrier_semaphore()
    peers = [device(y, 1 - c, z, x)] + [device(up(y, d), c, z, x) for d in (1, 2, 3)]
    peers += [device(y, c, up(z, dz), up(x, dx)) for dz, dx in OFFSETS]
    for peer in peers:
        pl.semaphore_signal(barrier, inc=1, device_id=peer, device_id_type=MESH)
    pl.semaphore_wait(barrier, len(peers))


class Ring:
    def __init__(self, block, half, place, p, sems, first):
        self.block, self.half, self.place, self.p = block, half, place, p
        self.sems, self.first = sems, first

    def start(self):
        p, b = self.p, self.block(self.p)
        self.right = rcopy(b, b, self.sems, self.first, self.place(up(p, 1)))
        self.left = rcopy(b, b, self.sems, self.first + 1, self.place(up(p, 3)))
        self.right.start()
        self.left.start()

    def relay(self):
        p = self.p
        self.right.wait_recv()
        h = self.half(up(p, 3), 0)
        self.on_right = rcopy(h, h, self.sems, self.first + 2, self.place(up(p, 1)))
        self.on_right.start()
        self.left.wait_recv()
        h = self.half(up(p, 1), 1)
        self.on_left = rcopy(h, h, self.sems, self.first + 3, self.place(up(p, 3)))
        self.on_left.start()

    def arrive(self):
        self.on_right.wait_recv()
        self.on_left.wait_recv()

    def finish(self):
        for copy in (self.right, self.left, self.on_right, self.on_left):
            copy.wait_send()


def gather_kernel(tok, cot, wqkv, wo, t_out, c_out, p_out, q_out, ss, sr, a2s, a2r, fs, fr, loc):
    y, c, z, x = coords()
    tm = z * 4 + x
    sib = device(y, 1 - c, z, x)
    greet(y, c, z, x)
    sems, a2, fw = (ss, sr), (a2s, a2r), (fs, fr)
    own = []
    for i, (src, dst) in enumerate(
        [(wqkv.at[c], p_out.at[:, y, c, z, x]), (wo, q_out.at[y, z, x]), (tok.at[tm], t_out.at[c, tm]), (cot.at[tm], c_out.at[c, tm])]
    ):
        copy = pltpu.make_async_copy(src, dst, loc.at[i])
        copy.start()
        own.append(copy)
    s0 = rcopy(wqkv.at[1 - c], p_out.at[:, y, c, z, x], sems, 0, sib)
    s0.start()
    tail = [s0]
    at_x = lambda v: device(y, c, z, v)
    at_y = lambda v: device(v, c, z, x)
    at_z = lambda v: device(y, c, v, x)
    n = 1
    px, pz, py = [], [], []
    for w in range(3):
        px.append(Ring(lambda v, w=w: p_out.at[w, y, :, z, v], lambda v, k, w=w: p_out.at[w, y, k, z, v], at_x, x, sems, n))
        pz.append(Ring(lambda v, w=w: p_out.at[w, y, :, v], lambda v, k, w=w: p_out.at[w, y, k, v], at_z, z, sems, n + 4))
        py.append(Ring(lambda v, w=w: p_out.at[w, v], lambda v, k, w=w: p_out.at[w, v, k], at_y, y, sems, n + 8))
        n += 12
    qy = Ring(lambda v: q_out.at[v, z, x], lambda v, k: q_out.at[v, z, x, :, pl.ds(1024 * k, 1024)], at_y, y, sems, n)
    qx = Ring(lambda v: q_out.at[:, z, v], lambda v, k: q_out.at[pl.ds(2 * k, 2), z, v], at_x, x, sems, n + 4)
    qz = Ring(lambda v: q_out.at[:, v], lambda v, k: q_out.at[pl.ds(2 * k, 2), v], at_z, z, sems, n + 8)

    own[1].wait()
    qy.start()
    own[0].wait()
    s0.wait_recv()
    for r in px:
        r.start()
    sends = []
    for i, (dz, dx) in enumerate(OFFSETS):
        zz, xx = up(z, dz), up(x, dx)
        for j, (src, dst) in enumerate([(tok, t_out), (cot, c_out)]):
            copy = rcopy(src.at[zz * 4 + xx], dst.at[c, tm], a2, 2 * i + j, device(y, c, zz, xx))
            sends.append(copy)
    for r in px:
        r.relay()
    qy.relay()
    for w in range(3):
        px[w].arrive()
        pz[w].start()
    qy.arrive()
    qx.start()
    for w in range(3):
        pz[w].relay()
    qx.relay()
    for w in range(3):
        pz[w].arrive()
        py[w].start()
    qx.arrive()
    qz.start()
    for copy in sends:
        copy.start()
    own[2].wait()
    own[3].wait()
    onward = []
    def pass_on(i, place):
        for j, buf in enumerate((t_out, c_out)):
            copy = rcopy(buf.at[c, place], buf.at[c, place], fw, 2 * i + j, sib)
            copy.start()
            onward.append(copy)
    pass_on(15, tm)
    def fwd(lo, hi):
        for i in range(lo, hi):
            dz, dx = OFFSETS[i]
            sends[2 * i].wait_recv()
            sends[2 * i + 1].wait_recv()
            pass_on(i, up(z, 4 - dz) * 4 + up(x, 4 - dx))
    fwd(0, 5)
    py[0].relay()
    fwd(5, 8)
    py[1].relay()
    qz.relay()
    fwd(8, 12)
    py[2].relay()
    fwd(12, 15)
    for w in range(3):
        py[w].arrive()
    qz.arrive()
    for copy in onward:
        copy.wait_recv()
    for copy in onward + sends + tail:
        copy.wait_send()
    for r in px + pz + py + [qy, qx, qz]:
        r.finish()

def gather_call(tok, cot, wqkv, wo):
    any_ = pl.BlockSpec(memory_space=pl.ANY)
    bf = jnp.bfloat16
    return pl.pallas_call(
        gather_kernel,
        out_shape=(
            jax.ShapeDtypeStruct((2, 16, 24, 2048), bf),
            jax.ShapeDtypeStruct((2, 16, 24, 2048), bf),
            jax.ShapeDtypeStruct((3, 4, 2, 4, 4, 16, 512), bf),
            jax.ShapeDtypeStruct((4, 4, 4, 8, 2048), bf),
        ),
        in_specs=[any_] * 4,
        out_specs=(any_,) * 4,
        scratch_shapes=[
            pltpu.SemaphoreType.DMA((49,)),
            pltpu.SemaphoreType.DMA((49,)),
            pltpu.SemaphoreType.DMA((30,)),
            pltpu.SemaphoreType.DMA((30,)),
            pltpu.SemaphoreType.DMA((32,)),
            pltpu.SemaphoreType.DMA((32,)),
            pltpu.SemaphoreType.DMA((4,)),
        ],
        compiler_params=pltpu.CompilerParams(collective_id=0, has_side_effects=True, vmem_limit_bytes=VMEM_LIMIT),
        name="gather",
    )(tok, cot, wqkv, wo)


def split_weights(w):
    return w.reshape(16, 4, 2, 128).transpose(2, 0, 1, 3).reshape(2, 16, 512)


def nt(a, b):
    return lax.dot_general(a, b, (((1,), (1,)), ((), ())), preferred_element_type=jnp.float32)


def tn(a, b):
    return lax.dot_general(a, b, (((0,), (0,)), ((), ())), preferred_element_type=jnp.float32)


def nn(a, b):
    return jnp.dot(a, b, preferred_element_type=jnp.float32)


FACTOR = 128 ** (-0.5)
BF = jnp.bfloat16
F32 = jnp.float32


def compute_kernel(t, c, w, wo, gain, mp, dp, gp, gq, gg, normed, scaled, proj, back, mask):
    rows_i = lax.broadcasted_iota(jnp.int32, (384, 384), 0)
    cols_i = lax.broadcasted_iota(jnp.int32, (384, 384), 1)
    same = lax.rem(rows_i + 384 - cols_i, 24) == 0
    mask[...] = jnp.where(same & (cols_i <= rows_i), 0.0, -1e30)

    @pl.loop(0, 12)
    def _(i):
        rows = pl.ds(pl.multiple_of(i * 64, 64), 64)
        x = t[rows, :].astype(F32)
        centered = x - jnp.mean(x, axis=-1, keepdims=True)
        inverse = lax.rsqrt(jnp.mean(centered * centered, axis=-1, keepdims=True) + 1e-05)
        s = centered * inverse
        scaled[rows, :] = s
        normed[rows, :] = (s * gain[...]).astype(BF)

    @pl.loop(0, 3)
    def _(i):
        rows = pl.ds(pl.multiple_of(i * 256, 256), 256)
        for k in range(3):
            proj[k, rows, :] = nn(normed[rows, :], w[k]).astype(BF)
        proj[3, rows, :] = nt(c[rows, :], wo[...]).astype(BF)

    @pl.loop(0, 8)
    def _(i):
        rows = pl.ds(pl.multiple_of(lax.div(i, 4) * 384, 128), 384)
        cols = pl.ds(pl.multiple_of(lax.rem(i, 4) * 128, 128), 128)
        q, k, v, u = (proj[j, rows, cols] for j in range(4))
        s = nt(q, k) * FACTOR + mask[...]
        e = jnp.exp(s - jnp.max(s, axis=-1, keepdims=True))
        p = e / jnp.sum(e, axis=-1, keepdims=True)
        p_b = p.astype(BF)
        back[3, rows, cols] = nn(p_b, v).astype(BF)
        d = nt(u, v)
        ds = (p * (d - jnp.sum(p * d, axis=-1, keepdims=True))).astype(BF)
        back[0, rows, cols] = (nn(ds, k) * FACTOR).astype(BF)
        back[1, rows, cols] = (tn(ds, q) * FACTOR).astype(BF)
        back[2, rows, cols] = tn(p_b, u).astype(BF)

    gg[...] = jnp.zeros_like(gg)

    @pl.loop(0, 3)
    def _(i):
        rows = pl.ds(pl.multiple_of(i * 256, 256), 256)
        mp[rows, :] = nn(back[3, rows, :], wo[...]).astype(BF)
        for h in range(2):
            half = pl.ds(h * 1024, 1024)
            dn = nt(back[0, rows, :], w[0, half, :])
            dn += nt(back[1, rows, :], w[1, half, :])
            dn += nt(back[2, rows, :], w[2, half, :])
            dp[rows, half] = dn.astype(BF)
            gg[:, half] += jnp.sum(dn * scaled[rows, half], axis=0, keepdims=True)

    @pl.loop(0, 8)
    def _(i):
        cols = pl.ds(pl.multiple_of(i * 256, 256), 256)
        left = normed[:, cols]
        for k in range(3):
            gp[k, cols, :] = tn(left, back[k]).astype(BF)

    @pl.loop(0, 2)
    def _(i):
        cols = pl.ds(pl.multiple_of(i * 256, 256), 256)
        gq[cols, :] = tn(back[3, :, cols], c[...]).astype(BF)


def compute_call(t, c, w, wo, gain):
    vm = pl.BlockSpec(memory_space=pltpu.VMEM)
    sds = jax.ShapeDtypeStruct
    return pl.pallas_call(
        compute_kernel,
        out_shape=(
            sds((768, 2048), BF),
            sds((768, 2048), BF),
            sds((3, 2048, 512), BF),
            sds((512, 2048), BF),
            sds((1, 2048), F32),
        ),
        in_specs=[vm] * 5,
        out_specs=(vm,) * 5,
        scratch_shapes=[
            pltpu.VMEM((768, 2048), BF),
            pltpu.VMEM((768, 2048), F32),
            pltpu.VMEM((4, 768, 512), BF),
            pltpu.VMEM((4, 768, 512), BF),
            pltpu.VMEM((384, 384), F32),
        ],
        compiler_params=pltpu.CompilerParams(vmem_limit_bytes=VMEM_LIMIT),
        name="attention",
    )(t, c, w, wo, gain)


class RingSum:
    def __init__(self, part, place, p, sems, first, via, land, total, units):
        self.part, self.place, self.p, self.sems, self.first = part, place, p, sems, first
        self.via, self.land, self.total, self.units = via, land, total, units

    def copy(self, i, src, dst, step):
        c = rcopy(src, dst, self.sems, self.first + i, self.place(up(self.p, step)))
        c.start()
        return c

    def start(self):
        p = self.p
        self.a = self.copy(0, self.part(up(p, 2), 0), self.via.at[0], 1)
        self.b = self.copy(1, self.part(up(p, 2), 1), self.via.at[1], 3)
        self.d = self.copy(2, self.part(up(p, 1), 1), self.land.at[0, 1], 1)
        self.e = self.copy(3, self.part(up(p, 3), 0), self.land.at[1, 0], 3)

    def add(self, out, terms):
        lead = out.shape[0]

        @pl.loop(0, lead)
        def _(i):
            value = terms[0][i].astype(F32)
            for term in terms[1:]:
                value = value + term[i].astype(F32)
            out[i] = value.astype(out.dtype)

    def relay(self):
        p = self.p
        self.a.wait_recv()
        self.add(self.via.at[2], [self.via.at[0], self.part(up(p, 1), 0)])
        self.f = self.copy(4, self.via.at[2], self.land.at[0, 0], 1)
        self.b.wait_recv()
        self.add(self.via.at[3], [self.via.at[1], self.part(up(p, 3), 1)])
        self.g = self.copy(5, self.via.at[3], self.land.at[1, 1], 3)

    def finish(self):
        for c in (self.d, self.e, self.f, self.g):
            c.wait_recv()
        for h in range(2):
            self.add(self.total(h), [self.part(self.p, h), self.land.at[0, h], self.land.at[1, h]])

    def drain(self):
        for c in (self.a, self.b, self.d, self.e, self.f, self.g):
            c.wait_send()


def scatter_kernel(t, c_in, mp, dp, gp, gq, gg, gain, mixed, grad, gw, go, gsum,
                   tv, cv, mr, dr, om, og,
                   pvia_y, pland_y, p1, pvia_z, pland_z, p2, pvia_x, pland_x, p3, p3r,
                   qvia_z, qland_z, q1, qvia_x, qland_x, q2, qvia_y, qland_y, q3,
                   gland, gacc, ss, sr, a2s, a2r, gs, gr, ms, mr_sem, loc):
    y, c, z, x = coords()
    tm = z * 4 + x
    sib = device(y, 1 - c, z, x)
    own = []
    for i, (src, dst) in enumerate([(t.at[c], tv), (c_in.at[c], cv)]):
        copy = pltpu.make_async_copy(src, dst, loc.at[i])
        copy.start()
        own.append(copy)
    greet(y, c, z, x)
    sems, a2, gsem, msem = (ss, sr), (a2s, a2r), (gs, gr), (ms, mr_sem)
    at_x = lambda v: device(y, c, z, v)
    at_y = lambda v: device(v, c, z, x)
    at_z = lambda v: device(y, c, v, x)
    swap = []
    for i, (src, dst) in enumerate([(mp, mr), (dp, dr)]):
        for h in range(2):
            rows = pl.ds(8 * h, 8)
            copy = rcopy(src.at[1 - c, rows], dst.at[rows], msem, 2 * i + h, sib)
            copy.start()
            swap.append(copy)
    py, pz, px = [], [], []
    n = 0
    for w in range(3):
        py.append(RingSum(lambda v, h, w=w: gp.at[w, v, h], at_y, y, sems, n, pvia_y.at[w], pland_y.at[w], lambda h, w=w: p1.at[w, h], 4))
        pz.append(RingSum(lambda v, h, w=w: p1.at[w, h, v], at_z, z, sems, n + 6, pvia_z.at[w], pland_z.at[w], lambda h, w=w: p2.at[w, h], 4))
        px.append(RingSum(lambda v, h, w=w: p2.at[w, h, pl.ds(v, 1)], at_x, x, sems, n + 12, pvia_x.at[w], pland_x.at[w], lambda h, w=w: p3.at[w, pl.ds(h, 1)], 1))
        n += 18
    qz = RingSum(lambda v, h: gq.at[pl.ds(2 * h, 2), v], at_z, z, sems, n, qvia_z, qland_z, lambda h: q1.at[pl.ds(2 * h, 2)], 2)
    qx = RingSum(lambda v, h: q1.at[pl.ds(2 * h, 2), v], at_x, x, sems, n + 6, qvia_x, qland_x, lambda h: q2.at[pl.ds(2 * h, 2)], 2)
    qy = RingSum(lambda v, h: q2.at[pl.ds(v, 1), :, pl.ds(1024 * h, 1024)], at_y, y, sems, n + 12, qvia_y, qland_y,
                 lambda h: q3.at[:, :, pl.ds(1024 * h, 1024)], 1)

    def gain_start(k, src):
        place, p = [(at_y, y), (at_z, z), (at_x, x)][k]
        out = []
        for d in (1, 2, 3):
            copy = rcopy(src, gland.at[3 * k + d - 1], gsem, 3 * k + d - 1, place(up(p, d)))
            copy.start()
            out.append(copy)
        return out

    def gain_finish(k, src, copies):
        for copy in copies:
            copy.wait_recv()
        gacc[k] = src[...] + gland[3 * k] + gland[3 * k + 1] + gland[3 * k + 2]

    g0 = gain_start(0, gg)
    for r in py:
        r.start()
    qz.start()
    own[0].wait()
    own[1].wait()
    sends = []

    def finalize(i, f):
        tok = tv[f].astype(F32)
        om[f] = (tok + (mp[c, f].astype(F32) + mr[f].astype(F32))).astype(BF)
        centered = tok - jnp.mean(tok, axis=-1, keepdims=True)
        inverse = lax.rsqrt(jnp.mean(centered * centered, axis=-1, keepdims=True) + 1e-05)
        s = centered * inverse
        ds = (dp[c, f].astype(F32) + dr[f].astype(F32)) * gain[...]
        first = jnp.mean(ds, axis=-1, keepdims=True)
        second = jnp.mean(ds * s, axis=-1, keepdims=True)
        og[f] = (inverse * (ds - first - s * second) + cv[f].astype(F32)).astype(BF)

    for copy in swap:
        copy.wait_recv()
    for i, (dz, dx) in enumerate(OFFSETS):
        zz, xx = up(z, dz), up(x, dx)
        f = zz * 4 + xx
        finalize(i, f)
        for j, (src, dst) in enumerate([(om, mixed), (og, grad)]):
            copy = rcopy(src.at[f], dst.at[tm], a2, 2 * i + j, device(y, c, zz, xx))
            copy.start()
            sends.append(copy)
    finalize(15, tm)
    mine = []
    for j, (src, dst) in enumerate([(om, mixed), (og, grad)]):
        copy = pltpu.make_async_copy(src.at[tm], dst.at[tm], loc.at[2 + j])
        copy.start()
        mine.append(copy)
    gain_finish(0, gg, g0)
    g1 = gain_start(1, gacc.at[0])
    py[0].relay()
    py[1].relay()
    qz.relay()
    py[2].relay()
    py[0].finish()
    pz[0].start()
    gain_finish(1, gacc.at[0], g1)
    g2 = gain_start(2, gacc.at[1])
    py[1].finish()
    pz[1].start()
    qz.finish()
    qx.start()
    pz[0].relay()
    py[2].finish()
    pz[2].start()
    qx.relay()
    pz[1].relay()
    pz[0].finish()
    px[0].start()
    pz[2].relay()
    qx.finish()
    qy.start()
    pz[1].finish()
    px[1].start()
    px[0].relay()
    gain_finish(2, gacc.at[1], g2)
    g3 = rcopy(gacc.at[2], gland.at[9], gsem, 9, sib)
    g3.start()
    pz[2].finish()
    px[2].start()
    qy.relay()
    px[1].relay()
    px[0].finish()
    px[2].relay()
    px[1].finish()
    qy.finish()
    px[2].finish()
    last = []
    for w in range(3):
        copy = rcopy(p3.at[w, 1 - c], p3r.at[w], msem, 4 + w, sib)
        copy.start()
        last.append(copy)
    go[...] = q3[0]
    g3.wait_recv()
    gsum[...] = gacc[2] + gland[9]
    for w in range(3):
        last[w].wait_recv()
        for j in range(4):
            cols = pl.ds(128 * j, 128)
            gw[w, :, pl.ds(pl.multiple_of((2 * j + c) * 128, 128), 128)] = p3[w, c, :, cols]
            gw[w, :, pl.ds(pl.multiple_of((2 * j + 1 - c) * 128, 128), 128)] = p3r[w, :, cols]
    for copy in mine:
        copy.wait()
    for copy in sends:
        copy.wait_recv()
    for copy in sends + swap + g0 + g1 + g2 + [g3] + last:
        copy.wait_send()
    for r in py + pz + px + [qz, qx, qy]:
        r.drain()


def scatter_call(t, c, mp, dp, gp, gq, gg, gain):
    vm = pl.BlockSpec(memory_space=pltpu.VMEM)
    any_ = pl.BlockSpec(memory_space=pl.ANY)
    sds = jax.ShapeDtypeStruct
    V = pltpu.VMEM
    sem = pltpu.SemaphoreType.DMA
    block = (16, 24, 2048)

    def ring(lead, unit):
        return [V(lead + (4,) + unit, BF), V(lead + (2, 2) + unit, BF)]

    return pl.pallas_call(
        scatter_kernel,
        out_shape=(
            sds(block, BF),
            sds(block, BF),
            sds((3, 16, 1024), F32),
            sds((8, 2048), F32),
            sds((16, 128), F32),
        ),
        in_specs=[any_, any_] + [vm] * 6,
        out_specs=(any_, any_, vm, vm, vm),
        scratch_shapes=[V(block, BF)] * 6
        + ring((3,), (4, 4, 16, 512))
        + [V((3, 2, 4, 4, 16, 512), BF)]
        + ring((3,), (4, 16, 512))
        + [V((3, 2, 4, 16, 512), BF)]
        + ring((3,), (1, 16, 512))
        + [V((3, 2, 16, 512), F32), V((3, 16, 512), F32)]
        + ring((), (2, 4, 8, 2048))
        + [V((4, 4, 8, 2048), BF)]
        + ring((), (2, 8, 2048))
        + [V((4, 8, 2048), BF)]
        + ring((), (1, 8, 1024))
        + [V((1, 8, 2048), F32)]
        + [V((10, 16, 128), F32), V((3, 16, 128), F32)]
        + [sem((72,)), sem((72,)), sem((30,)), sem((30,)), sem((10,)), sem((10,)), sem((7,)), sem((7,)), sem((4,))],
        compiler_params=pltpu.CompilerParams(collective_id=1, has_side_effects=True, vmem_limit_bytes=VMEM_LIMIT),
        name="scatter",
    )(t, c, mp, dp, gp, gq, gg, gain)


def on_device(tokens, cotangent, norm_gain, w_query, w_key, w_value, w_out):
    tok = tokens.reshape(16, 24, 2048)
    cot = cotangent.reshape(16, 24, 2048)
    wqkv = jnp.stack([split_weights(w) for w in (w_query, w_key, w_value)], axis=1)
    t, c, wp, wq = gather_call(tok, cot, wqkv, w_out)
    gain = norm_gain.astype(F32).reshape(1, 2048)
    mp, dp, gp, gq, gg = compute_call(
        t.reshape(768, 2048), c.reshape(768, 2048), wp.reshape(3, 2048, 512), wq.reshape(512, 2048), gain
    )
    mixed, grad, gw, go, gsum = scatter_call(
        t,
        c,
        mp.reshape(2, 16, 24, 2048),
        dp.reshape(2, 16, 24, 2048),
        gp.reshape(3, 4, 2, 4, 4, 16, 512),
        gq.reshape(4, 4, 4, 8, 2048),
        gg.reshape(16, 128),
        gain,
    )
    index = lax.axis_index("dp") * 16 + lax.axis_index("tm")
    grad_gain = lax.dynamic_index_in_dim(gsum.reshape(128, 16), index, 0, keepdims=False)
    shape = (1, 1, 384, 2048)
    return mixed.reshape(shape), grad.reshape(shape), grad_gain, gw[0], gw[1], gw[2], go


def solution(mesh):
    rows = P("dp", "tm", None, None)
    weight = P(("dp", "tm"), None)
    return jax.shard_map(
        on_device,
        mesh=mesh,
        in_specs=(rows, rows, P()) + (weight,) * 4,
        out_specs=(rows, rows, P(("dp", "tm"))) + (weight,) * 4,
        check_vma=False,
    )
```

time: 815 us -> 234 us (0.29); the launches traced: 804 us -> 233 us
  waiting for transfers between devices: 470 us -> 0 us
  Pallas kernels: 0 us -> 222 us
  blocking collectives: 126 us -> 0 us
  matrix products: 69.5 us -> 0 us
  local copies, waits for them, and re-layouts: 66.8 us -> 9.93 us
  other arithmetic: 39.8 us -> 1.26 us
  between operations: 17 us -> 0.74 us
  starting transfers between devices: 15 us -> 0 us
    reduce_scatter x7 -> x0, waiting for transfers between devices: 238 us -> none  [the longest x1 73.6 us: on_device(): lax.psum_scatter(partial_sums[2].astype(jnp.bfloat16), 'tm', scatter_dime...]
    pallas_call x0 -> x3, Pallas kernels: none -> 222 us  [the longest x1 91.2 us: scatter_call(): pl.pallas_call(scatter_kernel, out_shape=(sds(block, BF), sds(block, BF),...]
    all_gather x4 -> x0, waiting for transfers between devices: 168 us -> none  [the longest x1 67.4 us: on_device(): lax.all_gather(w_value, ('dp', 'tm'), axis=0, tiled=True)]
    all_to_all x5 -> x0, blocking collectives: 77.4 us -> none  [the longest x1 19.7 us: on_device(): lax.all_to_all(attended[0], 'tm', split_axis=0, concat_axis=1, tiled=True)]
    dot_general x17 -> x0, matrix products: 65.4 us -> none  [the longest x4 19.4 us: transpose_dot(): lax.dot_general(left, right, (((0,), (0,)), ((), ())), preferred_element_...]
    unnamed x13 -> x0, waiting for transfers between devices: 64.4 us -> none
    unnamed x2 -> x0, blocking collectives: 49 us -> none
    unnamed x54 -> x9, local copies, waits for them, and re-layouts: 40.6 us -> 4.51 us
  transfers between devices with their start and end apart: 15 -> 0, of which waited for: 8 -> 0; matrix products, arithmetic and copies ran while one was open for 21% -> 0% of each run, Pallas kernels for 0% -> 0%
where the time goes in v1:
time: 234 us; the launch traced here: 233 us
  Pallas kernels  222 us (95%)
  local copies, waits for them, and re-layouts  9.93 us (4%)
    pallas_call x1, Pallas kernels, scatter_call(): pl.pallas_call(scatter_kernel, out_shape=(sds(block, BF), sds(block, BF),...  91.2 us
    pallas_call x1, Pallas kernels, gather_call(): pl.pallas_call(gather_kernel, out_shape=(jax.ShapeDtypeStruct((2, 16, 24,...  86 us
    pallas_call x1, Pallas kernels, compute_call(): pl.pallas_call(compute_kernel, out_shape=(sds((768, 2048), BF), sds((768,...  44.3 us

profile of v1, /device:TPU:1, one launch (start us, length us, event | category | flops | bytes accessed | tf_op | source)
XLA Modules:
  0.0 233.4 jit_solution(4303108053295900629)
XLA Ops:
  0.6 0.0 copy-start.2
  0.6 0.8 reshape.73
  1.5 0.8 reshape.74
  2.3 0.8 reshape.72
  3.1 0.7 pad_maximum_fusion.wqkv
  3.8 86.0 %gather.1 = (bf16[2,16,24,2048]{3,2,1,0:T(8,128)(2,1)}, bf16[2,16,24,2048]{3,2,1,0:T(8,128)(2,1)}, bf16[3,4,2,4,4,16,512]{6,5,4,3,2,1,0:T(8,128)(2,1)}, bf16[4,4,4,8,2048]{4,3,2,1,0:T(8,128)(2,1)}) custom-call(bf16[16,24,2048]{2,1,0:T(8,128)(2,1)} %bitcast.39, bf16[16,24,2048]{2,1,0:T(8,128)(2,1)} %bitcast.40, bf16[2,3,16,512]{3,2,1,0:T(8,128)(2,1)} %pad_maximum_fusion.wqkv, ...), custom_call_target="tpu_custom_call" | custom-call | tf_op jit(solution)/shard_map/gather/pallas_call | solution.py:181
  89.8 0.0 copy-done.2
  89.8 0.6 reshape.89
  90.4 44.3 %attention.1 = (bf16[768,2048]{1,0:T(8,128)(2,1)}, bf16[768,2048]{1,0:T(8,128)(2,1)}, bf16[3,2048,512]{2,1,0:T(8,128)(2,1)}, bf16[512,2048]{1,0:T(8,128)(2,1)}, f32[1,2048]{1,0:T(1,128)}) custom-call(bf16[768,2048]{1,0:T(8,128)(2,1)} %bitcast.31, bf16[768,2048]{1,0:T(8,128)(2,1)} %bitcast.32, bf16[3,2048,512]{2,1,0:T(8,128)(2,1)} %bitcast.33, ...), custom_call_target="tpu_custom_call" | custom-call | tf_op jit(solution)/shard_map/attention/pallas_call | solution.py:295
  134.7 91.2 %scatter.1 = (bf16[16,24,2048]{2,1,0:T(8,128)(2,1)}, bf16[16,24,2048]{2,1,0:T(8,128)(2,1)}, f32[3,16,1024]{2,1,0:T(8,128)}, f32[8,2048]{1,0:T(8,128)}, f32[16,128]{1,0:T(8,128)}) custom-call(bf16[2,16,24,2048]{3,2,1,0:T(8,128)(2,1)} %get-tuple-element.21.t, bf16[2,16,24,2048]{3,2,1,0:T(8,128)(2,1)} %get-tuple-element.22.c_in, ...), custom_call_target="tpu_custom_call" | custom-call | tf_op jit(solution)/shard_map/scatter/pallas_call | solution.py:525
  225.9 0.0 copy-start
  225.9 1.7 slice_bitcast_fusion
  227.6 0.8 reshape.88
  228.4 0.5 dynamic-slice_bitcast_fusion
  228.9 2.7 %copy.29 = bf16[1,1,384,2048]{3,2,1,0:T(8,128)(2,1)} copy(bf16[1,1,384,2048]{3,2,1,0:T(8,128)(2,1)} %bitcast.42) | data formatting | bytes 3145728
  231.7 0.0 copy-done
  231.7 0.0 copy-start.1
  231.7 1.1 copy.30
  232.8 0.0 copy-done.1
  232.8 0.6 copy.31
  (6 shorter events, 0.1 us)
Async XLA Ops:
  0.6 89.1 %copy-start.2 = (bf16[2048]{0:T(1024)(128)(2,1)S(1)}, bf16[2048]{0:T(1024)(128)(2,1)}, u32[]{:S(2)}) copy-start(bf16[2048]{0:T(1024)(128)(2,1)} %param.9) | copy-start | bytes 12292
  225.9 5.7 %copy-start = (bf16[16,24,2048]{2,1,0:T(8,128)(2,1)S(1)}, bf16[16,24,2048]{2,1,0:T(8,128)(2,1)}, u32[]{:S(2)}) copy-start(bf16[16,24,2048]{2,1,0:T(8,128)(2,1)} %get-tuple-element.31) | copy-start | bytes 4718596
  231.7 1.1 copy-start.1

commit v2 on v0

v2 whole, which is shorter than its diff:
```python
import functools

import jax
import jax.numpy as jnp
from jax import lax
from jax.experimental import pallas as pl
from jax.experimental.pallas import tpu as pltpu
from jax.sharding import PartitionSpec as P

MESH = pl.DeviceIdType.MESH
VMEM_LIMIT = 62 * 1024 * 1024


def coords():
    dp, tm = lax.axis_index("dp"), lax.axis_index("tm")
    return lax.div(dp, 2), lax.rem(dp, 2), lax.div(tm, 4), lax.rem(tm, 4)


def device(y, c, z, x):
    return {"dp": y * 2 + c, "tm": z * 4 + x}


def up(p, d):
    return lax.rem(p + d, 4)


def rcopy(src, dst, sems, i, where):
    return pltpu.make_async_remote_copy(
        src_ref=src,
        dst_ref=dst,
        send_sem=sems[0].at[i],
        recv_sem=sems[1].at[i],
        device_id=where,
        device_id_type=MESH,
    )


OFFSETS = [
    (0, 1), (0, 3), (1, 0), (3, 0), (1, 1), (3, 3), (1, 3), (3, 1),
    (2, 2), (0, 2), (2, 0), (2, 1), (2, 3), (1, 2), (3, 2),
]


def greet(y, c, z, x, tm_peers=True):
    barrier = pltpu.get_barrier_semaphore()
    peers = [device(y, 1 - c, z, x)] + [device(up(y, d), c, z, x) for d in (1, 2, 3)]
    peers += [device(y, c, up(z, dz), up(x, dx)) for dz, dx in OFFSETS]
    for peer in peers:
        pl.semaphore_signal(barrier, inc=1, device_id=peer, device_id_type=MESH)
    pl.semaphore_wait(barrier, len(peers))


class Ring:
    def __init__(self, block, half, place, p, sems, first):
        self.block, self.half, self.place, self.p = block, half, place, p
        self.sems, self.first = sems, first

    def start(self):
        p, b = self.p, self.block(self.p)
        self.right = rcopy(b, b, self.sems, self.first, self.place(up(p, 1)))
        self.left = rcopy(b, b, self.sems, self.first + 1, self.place(up(p, 3)))
        self.right.start()
        self.left.start()

    def relay(self):
        p = self.p
        self.right.wait_recv()
        h = self.half(up(p, 3), 0)
        self.on_right = rcopy(h, h, self.sems, self.first + 2, self.place(up(p, 1)))
        self.on_right.start()
        self.left.wait_recv()
        h = self.half(up(p, 1), 1)
        self.on_left = rcopy(h, h, self.sems, self.first + 3, self.place(up(p, 3)))
        self.on_left.start()

    def arrive(self):
        self.on_right.wait_recv()
        self.on_left.wait_recv()

    def finish(self):
        for copy in (self.right, self.left, self.on_right, self.on_left):
            copy.wait_send()


def nt(a, b):
    return lax.dot_general(a, b, (((1,), (1,)), ((), ())), preferred_element_type=jnp.float32)


def tn(a, b):
    return lax.dot_general(a, b, (((0,), (0,)), ((), ())), preferred_element_type=jnp.float32)


def nn(a, b):
    return jnp.dot(a, b, preferred_element_type=jnp.float32)


FACTOR = 128 ** (-0.5)
BF = jnp.bfloat16
F32 = jnp.float32


class RingSum:
    def __init__(self, part, place, p, sems, first, via, land, total):
        self.part, self.place, self.p, self.sems, self.first = part, place, p, sems, first
        self.via, self.land, self.total = via, land, total

    def copy(self, i, src, dst, step):
        c = rcopy(src, dst, self.sems, self.first + i, self.place(up(self.p, step)))
        c.start()
        return c

    def start(self):
        p = self.p
        self.a = self.copy(0, self.part(up(p, 2), 0), self.via.at[0], 1)
        self.b = self.copy(1, self.part(up(p, 2), 1), self.via.at[1], 3)
        self.d = self.copy(2, self.part(up(p, 1), 1), self.land.at[0, 1], 1)
        self.e = self.copy(3, self.part(up(p, 3), 0), self.land.at[1, 0], 3)

    def add(self, out, terms):
        lead = out.shape[0]

        @pl.loop(0, lead)
        def _(i):
            value = terms[0][i].astype(F32)
            for term in terms[1:]:
                value = value + term[i].astype(F32)
            out[i] = value.astype(out.dtype)

    def relay(self):
        p = self.p
        self.a.wait_recv()
        self.add(self.via.at[2], [self.via.at[0], self.part(up(p, 1), 0)])
        self.f = self.copy(4, self.via.at[2], self.land.at[0, 0], 1)
        self.b.wait_recv()
        self.add(self.via.at[3], [self.via.at[1], self.part(up(p, 3), 1)])
        self.g = self.copy(5, self.via.at[3], self.land.at[1, 1], 3)

    def finish(self):
        for c in (self.d, self.e, self.f, self.g):
            c.wait_recv()
        for h in range(2):
            self.add(self.total(h), [self.part(self.p, h), self.land.at[0, h], self.land.at[1, h]])

    def drain(self):
        for c in (self.a, self.b, self.d, self.e, self.f, self.g):
            c.wait_send()


def wait_bytes(ref, sem):
    pltpu.make_async_copy(ref, ref, sem).wait()


def block_kernel(tok, cot, wq, wk, wv, w_out, gain, mixed, grad, g_q, g_k, g_v, g_o, gsum,
                 t, ct, w, wo, wom, normed, cotm, scaled, proj, back, mask, mp, dp, mr, dr, om, og,
                 via1, land1, sum1, via2, land2, sum2, via3, land3, p3, p3r,
                 qvia1, qland1, q1, qvia2, qland2, q2, qvia3, qland3, q3,
                 gg, gland, gacc,
                 ag_s, ag_r, w_s, w_r, w_l, in_s, in_r, fw_s, fw_r, sw_s, sw_r, bk_s, bk_r, rs_s, rs_r, gn_s, gn_r, loc):
    y, c, z, x = coords()
    tm = z * 4 + x
    sib = device(y, 1 - c, z, x)
    at_x = lambda v: device(y, c, z, v)
    at_y = lambda v: device(v, c, z, x)
    at_z = lambda v: device(y, c, v, x)

    stage = []
    for j, (src, dst) in enumerate([(tok, om), (cot, og)]):
        for g in range(3):
            copy = pltpu.make_async_copy(src.at[:, g], dst.at[g], loc.at[3 * j + g])
            copy.start()
            stage.append(copy)
    own_o = pltpu.make_async_copy(w_out, wo.at[y, z, x], loc.at[6])
    own_o.start()
    own_w = []
    for i, src in enumerate((wq, wk, wv)):
        for j in range(4):
            cols = pl.ds(pl.multiple_of((2 * j + c) * 128, 128), 128)
            copy = pltpu.make_async_copy(src.at[:, cols], w.at[i, y, c, z, x, :, pl.ds(128 * j, 128)], w_l.at[4 * i + j])
            copy.start()
            own_w.append(copy)
    greet(y, c, z, x)

    swap_w = []
    for i, src in enumerate((wq, wk, wv)):
        for j in range(4):
            cols = pl.ds(pl.multiple_of((2 * j + 1 - c) * 128, 128), 128)
            copy = rcopy(src.at[:, cols], w.at[i, y, c, z, x, :, pl.ds(128 * j, 128)], (w_s, w_r), 4 * i + j, sib)
            copy.start()
            swap_w.append(copy)

    ag = (ag_s, ag_r)

    def yx(i):
        a = Ring(lambda v: w.at[i, y, :, z, v], lambda v, k: w.at[i, y, k, z, v], at_x, x, ag, 12 * i)
        b = Ring(lambda v: w.at[i, y, :, v], lambda v, k: w.at[i, y, k, v], at_z, z, ag, 12 * i + 4)
        d = Ring(lambda v: w.at[i, v], lambda v, k: w.at[i, v, k], at_y, y, ag, 12 * i + 8)
        return a, b, d

    qa, qb, qc = yx(0)
    ka, kb, kc = yx(1)
    va = Ring(lambda v: w.at[2, v, :, z, x], lambda v, k: w.at[2, v, k, z, x], at_y, y, ag, 24)
    vb = Ring(lambda v: w.at[2, :, :, v, x], lambda v, k: w.at[2, :, k, v, x], at_z, z, ag, 28)
    vc = Ring(lambda v: w.at[2, :, :, :, v], lambda v, k: w.at[2, :, k, :, v], at_x, x, ag, 32)
    oa = Ring(lambda v: wo.at[v, z, x], lambda v, k: wo.at[v, z, x, :, pl.ds(1024 * k, 1024)], at_y, y, ag, 36)
    ob = Ring(lambda v: wo.at[:, z, v], lambda v, k: wo.at[pl.ds(2 * k, 2), z, v], at_x, x, ag, 40)
    oc = Ring(lambda v: wo.at[:, v], lambda v, k: wo.at[pl.ds(2 * k, 2), v], at_z, z, ag, 44)
    rings = (qa, qb, qc, ka, kb, kc, va, vb, vc, oa, ob, oc)

    own_o.wait()
    oa.start()
    for copy in own_w:
        copy.wait()
    for copy in swap_w:
        copy.wait_recv()
    for r in (qa, va, ka):
        r.start()

    def spread(g):
        for j, (src, staged, dst) in enumerate([(tok, om, t), (cot, og, ct)]):
            stage[3 * j + g].wait()
            pltpu.make_async_copy(src.at[tm, g], dst.at[c, g, tm], in_r.at[2 * g + j]).start()
        for dz, dx in OFFSETS:
            zz, xx = up(z, dz), up(x, dx)
            for j, (staged, dst) in enumerate([(om, t), (og, ct)]):
                rcopy(staged.at[g, zz * 4 + xx], dst.at[c, g, tm], (in_s, in_r), 2 * g + j, device(y, c, zz, xx)).start()

    passed = {}

    def pass_on(g):
        passed[g] = []
        for j, dst in enumerate((t, ct)):
            wait_bytes(dst.at[c, g], in_r.at[2 * g + j])
            copy = rcopy(dst.at[c, g], dst.at[c, g], (fw_s, fw_r), 2 * g + j, sib)
            copy.start()
            passed[g].append(copy)

    def norm(g):
        for copy in passed[g]:
            copy.wait_recv()

        @pl.loop(0, 8)
        def _(i):
            k, f = lax.div(i, 4), lax.rem(i, 4) * 4
            value = t[k, g, pl.ds(f, 4)].astype(F32).reshape(32, 2048)
            centered = value - jnp.mean(value, axis=-1, keepdims=True)
            inverse = lax.rsqrt(jnp.mean(centered * centered, axis=-1, keepdims=True) + 1e-05)
            s = centered * inverse
            scaled[pl.ds(pl.multiple_of(i * 32, 32), 32), :] = s
            rows = pl.ds(pl.multiple_of(g * 256 + i * 32, 32), 32)
            normed[rows, :] = (s * gain[...]).astype(BF)
            cotm[rows, :] = ct[k, g, pl.ds(f, 4)].astype(F32).reshape(32, 2048).astype(BF)

    def project(g, i):
        rows = pl.ds(g * 256, 256)
        if i < 3:
            proj[i] = nn(normed[rows, :], w[i].reshape(2048, 512)).astype(BF)
        else:
            proj[3] = nt(cotm[rows, :], wom[...]).astype(BF)

    def attention(g):
        @pl.loop(0, 4)
        def _(h):
            cols = pl.ds(pl.multiple_of(h * 128, 128), 128)
            for clip in range(2):
                rows = pl.ds(clip * 128, 128)
                out = pl.ds(g * 256 + clip * 128, 128)
                q, k, v, u = (proj[j, rows, cols] for j in range(4))
                s = nt(q, k) * FACTOR + mask[...]
                e = jnp.exp(s - jnp.max(s, axis=-1, keepdims=True))
                p = e / jnp.sum(e, axis=-1, keepdims=True)
                p_b = p.astype(BF)
                back[3, out, cols] = nn(p_b, v).astype(BF)
                d = nt(u, v)
                ds = (p * (d - jnp.sum(p * d, axis=-1, keepdims=True))).astype(BF)
                back[0, out, cols] = (nn(ds, k) * FACTOR).astype(BF)
                back[1, out, cols] = (tn(ds, q) * FACTOR).astype(BF)
                back[2, out, cols] = tn(p_b, u).astype(BF)

    swapped = {}

    def partials(g):
        rows = pl.ds(g * 256, 256)
        for h in range(2):
            half = pl.ds(h * 1024, 1024)
            mp[g, :, :, :, half] = nn(back[3, rows, :], wom[:, half]).reshape(2, 16, 8, 1024).astype(BF)
            dn = None
            for i in range(3):
                term = nt(back[i, rows, :], w[i, pl.ds(2 * h, 2)].reshape(1024, 512))
                dn = term if dn is None else dn + term
            dp[g, :, :, :, half] = dn.reshape(2, 16, 8, 1024).astype(BF)
            total = jnp.sum(dn * scaled[:, half], axis=0, keepdims=True)
            gg[:, half] = total if g == 0 else gg[:, half] + total
        swapped[g] = []
        for j, (src, dst) in enumerate([(mp, mr), (dp, dr)]):
            copy = rcopy(src.at[g, 1 - c], dst.at[g], (sw_s, sw_r), 2 * g + j, sib)
            copy.start()
            swapped[g].append(copy)

    def finalize(g):
        for j, staged in enumerate((om, og)):
            wait_bytes(staged.at[g, pl.ds(0, 15)], in_s.at[2 * g + j])
        for copy in swapped[g]:
            copy.wait_recv()

        @pl.loop(0, 4)
        def _(i):
            fs = pl.ds(i * 4, 4)
            value = t[c, g, fs].astype(F32)
            om[g, fs] = (value + (mp[g, c, fs].astype(F32) + mr[g, fs].astype(F32))).astype(BF)
            centered = value - jnp.mean(value, axis=-1, keepdims=True)
            inverse = lax.rsqrt(jnp.mean(centered * centered, axis=-1, keepdims=True) + 1e-05)
            s = centered * inverse
            ds = (dp[g, c, fs].astype(F32) + dr[g, fs].astype(F32)) * gain[...].reshape(1, 1, 2048)
            first = jnp.mean(ds, axis=-1, keepdims=True)
            second = jnp.mean(ds * s, axis=-1, keepdims=True)
            og[g, fs] = (inverse * (ds - first - s * second) + ct[c, g, fs].astype(F32)).astype(BF)

        for dz, dx in OFFSETS:
            zz, xx = up(z, dz), up(x, dx)
            for j, (src, dst) in enumerate([(om, mixed), (og, grad)]):
                rcopy(src.at[g, zz * 4 + xx], dst.at[tm, g], (bk_s, bk_r), j, device(y, c, zz, xx)).start()
        for j, (src, dst) in enumerate([(om, mixed), (og, grad)]):
            pltpu.make_async_copy(src.at[g, tm], dst.at[tm, g], bk_r.at[j]).start()

    def w_terms(i):
        @pl.loop(0, 8)
        def _(b):
            cols = pl.ds(pl.multiple_of(b * 256, 256), 256)
            w[i, lax.div(b, 2), lax.rem(b, 2)] = tn(normed[:, cols], back[i]).reshape(4, 4, 16, 512).astype(BF)

    def o_terms():
        @pl.loop(0, 2)
        def _(b):
            cols = pl.ds(pl.multiple_of(b * 256, 256), 256)
            wo[pl.ds(2 * b, 2)] = tn(back[3, :, cols], cotm[...]).reshape(2, 4, 4, 8, 2048).astype(BF)

    rs = (rs_s, rs_r)

    def sums(i):
        if i < 2:
            a = RingSum(lambda v, h: w.at[i, v, h], at_y, y, rs, 18 * i, via1.at[i], land1.at[i], lambda h: sum1.at[i, h])
            b = RingSum(lambda v, h: sum1.at[i, h, v], at_z, z, rs, 18 * i + 6, via2.at[i], land2.at[i], lambda h: sum2.at[i, h])
            d = RingSum(lambda v, h: sum2.at[i, h, pl.ds(v, 1)], at_x, x, rs, 18 * i + 12, via3.at[i], land3.at[i],
                        lambda h: p3.at[i, pl.ds(h, 1)])
        else:
            a = RingSum(lambda v, h: w.at[i, :, h, :, v], at_x, x, rs, 18 * i, via1.at[i], land1.at[i], lambda h: sum1.at[i, h])
            b = RingSum(lambda v, h: sum1.at[i, h, :, v], at_z, z, rs, 18 * i + 6, via2.at[i], land2.at[i], lambda h: sum2.at[i, h])
            d = RingSum(lambda v, h: sum2.at[i, h, pl.ds(v, 1)], at_y, y, rs, 18 * i + 12, via3.at[i], land3.at[i],
                        lambda h: p3.at[i, pl.ds(h, 1)])
        return a, b, d

    qx, qy, qz = sums(0)
    kx, ky, kz = sums(1)
    vx, vy, vz = sums(2)
    ox = RingSum(lambda v, h: wo.at[pl.ds(2 * h, 2), v], at_z, z, rs, 54, qvia1, qland1, lambda h: q1.at[pl.ds(2 * h, 2)])
    oy = RingSum(lambda v, h: q1.at[pl.ds(2 * h, 2), v], at_x, x, rs, 60, qvia2, qland2, lambda h: q2.at[pl.ds(2 * h, 2)])
    oz = RingSum(lambda v, h: q2.at[pl.ds(v, 1), :, pl.ds(1024 * h, 1024)], at_y, y, rs, 66, qvia3, qland3,
                 lambda h: q3.at[:, :, pl.ds(1024 * h, 1024)])
    all_sums = (qx, qy, qz, kx, ky, kz, vx, vy, vz, ox, oy, oz)

    def gain_start(k, src):
        place, p = [(at_y, y), (at_z, z), (at_x, x)][k]
        out = []
        for d in (1, 2, 3):
            copy = rcopy(src, gland.at[3 * k + d - 1], (gn_s, gn_r), 3 * k + d - 1, place(up(p, d)))
            copy.start()
            out.append(copy)
        return out

    def gain_finish(k, src, copies):
        for copy in copies:
            copy.wait_recv()
        gacc[k] = src[...] + gland[3 * k] + gland[3 * k + 1] + gland[3 * k + 2]

    spread(0)
    rows_i = lax.broadcasted_iota(jnp.int32, (128, 128), 0)
    cols_i = lax.broadcasted_iota(jnp.int32, (128, 128), 1)
    same = lax.rem(rows_i + 128 - cols_i, 8) == 0
    mask[...] = jnp.where(same & (cols_i <= rows_i), 0.0, -1e30)
    for r in (qa, oa, va, ka):
        r.relay()
    for a, b in ((qa, qb), (oa, ob), (va, vb), (ka, kb)):
        a.arrive()
        b.start()
    for r in (qb, ob, vb, kb):
        r.relay()
    for a, b in ((qb, qc), (ob, oc), (vb, vc), (kb, kc)):
        a.arrive()
        b.start()
    pass_on(0)
    norm(0)
    qc.relay()
    vc.relay()
    oc.relay()
    spread(1)
    kc.relay()
    spread(2)
    qc.arrive()
    project(0, 0)
    vc.arrive()
    project(0, 2)
    oc.arrive()

    @pl.loop(0, 4)
    def _(j):
        wom[pl.ds(pl.multiple_of(j * 128, 128), 128), :] = wo[j].astype(F32).reshape(128, 2048).astype(BF)

    project(0, 3)
    kc.arrive()
    project(0, 1)
    attention(0)
    pass_on(1)
    partials(0)
    norm(1)
    for i in range(4):
        project(1, i)
    finalize(0)
    attention(1)
    pass_on(2)
    partials(1)
    norm(2)
    for i in range(4):
        project(2, i)
    finalize(1)
    attention(2)
    partials(2)
    for i in range(16):
        gland[9, pl.ds(i, 1), :] = gg[:, pl.ds(128 * i, 128)]
    g0 = gain_start(0, gland.at[9])
    for r in rings:
        r.finish()
    w_terms(1)
    kx.start()
    w_terms(2)
    vx.start()
    finalize(2)
    o_terms()
    ox.start()
    kx.relay()
    w_terms(0)
    qx.start()
    vx.relay()
    ox.relay()
    gain_finish(0, gland.at[9], g0)
    g1 = gain_start(1, gacc.at[0])
    kx.finish()
    ky.start()
    qx.relay()
    vx.finish()
    vy.start()
    ox.finish()
    oy.start()
    ky.relay()
    gain_finish(1, gacc.at[0], g1)
    g2 = gain_start(2, gacc.at[1])
    vy.relay()
    oy.relay()
    ky.finish()
    kz.start()
    qx.finish()
    qy.start()
    vy.finish()
    vz.start()
    oy.finish()
    oz.start()
    kz.relay()
    vz.relay()
    oz.relay()
    qy.relay()
    gain_finish(2, gacc.at[1], g2)
    g3 = rcopy(gacc.at[2], gland.at[10], (gn_s, gn_r), 9, sib)
    g3.start()
    last = {}

    def across(i):
        copy = rcopy(p3.at[i, 1 - c], p3r.at[i], (sw_s, sw_r), 6 + i, sib)
        copy.start()
        last[i] = copy

    def put(i, out):
        last[i].wait_recv()
        for j in range(4):
            cols = pl.ds(128 * j, 128)
            out[:, pl.ds(pl.multiple_of((2 * j + c) * 128, 128), 128)] = p3[i, c, :, cols]
            out[:, pl.ds(pl.multiple_of((2 * j + 1 - c) * 128, 128), 128)] = p3r[i, :, cols]

    kz.finish()
    across(1)
    qy.finish()
    qz.start()
    vz.finish()
    across(2)
    oz.finish()
    g_o[...] = q3[0]
    put(1, g_k)
    qz.relay()
    put(2, g_v)
    g3.wait_recv()
    gsum[...] = gacc[2] + gland[10]
    qz.finish()
    across(0)
    put(0, g_q)
    for j, (src, dst) in enumerate([(om, mixed), (og, grad)]):
        wait_bytes(dst, bk_r.at[j])
        wait_bytes(src.at[:, pl.ds(0, 15)], bk_s.at[j])
    for copies in (swap_w, passed[0], passed[1], passed[2], swapped[0], swapped[1], swapped[2], g0, g1, g2, [g3], list(last.values())):
        for copy in copies:
            copy.wait_send()
    for r in all_sums:
        r.drain()


def block_call(tok, cot, wq, wk, wv, w_out, gain):
    vm = pl.BlockSpec(memory_space=pltpu.VMEM)
    any_ = pl.BlockSpec(memory_space=pl.ANY)
    sds = jax.ShapeDtypeStruct
    V = pltpu.VMEM
    sem = pltpu.SemaphoreType.DMA
    rows = (16, 3, 8, 2048)
    groups = (3, 16, 8, 2048)

    def ring(lead, unit):
        return [V(lead + (4,) + unit, BF), V(lead + (2, 2) + unit, BF)]

    sems = [48, 48, 12, 12, 12, 6, 6, 6, 6, 9, 9, 2, 2, 72, 72, 10, 10, 7]
    return pl.pallas_call(
        block_kernel,
        out_shape=(sds(rows, BF), sds(rows, BF))
        + (sds((16, 1024), F32),) * 3
        + (sds((8, 2048), F32), sds((16, 128), F32)),
        in_specs=[any_] * 6 + [vm],
        out_specs=(any_, any_) + (vm,) * 5,
        scratch_shapes=[V((2, 3, 16, 8, 2048), BF)] * 2
        + [V((3, 4, 2, 4, 4, 16, 512), BF), V((4, 4, 4, 8, 2048), BF), V((512, 2048), BF)]
        + [V((768, 2048), BF)] * 2
        + [V((256, 2048), F32), V((4, 256, 512), BF), V((4, 768, 512), BF), V((128, 128), F32)]
        + [V((3, 2, 16, 8, 2048), BF)] * 2
        + [V(groups, BF)] * 4
        + ring((3,), (4, 4, 16, 512))
        + [V((3, 2, 4, 4, 16, 512), BF)]
        + ring((3,), (4, 16, 512))
        + [V((3, 2, 4, 16, 512), BF)]
        + ring((3,), (1, 16, 512))
        + [V((3, 2, 16, 512), F32), V((3, 16, 512), F32)]
        + ring((), (2, 4, 8, 2048))
        + [V((4, 4, 8, 2048), BF)]
        + ring((), (2, 8, 2048))
        + [V((4, 8, 2048), BF)]
        + ring((), (1, 8, 1024))
        + [V((1, 8, 2048), F32)]
        + [V((1, 2048), F32), V((11, 16, 128), F32), V((3, 16, 128), F32)]
        + [sem((n,)) for n in sems],
        compiler_params=pltpu.CompilerParams(collective_id=0, has_side_effects=True, vmem_limit_bytes=VMEM_LIMIT),
        name="block",
    )(tok, cot, wq, wk, wv, w_out, gain)


def on_device(tokens, cotangent, norm_gain, w_query, w_key, w_value, w_out):
    tok = tokens.reshape(16, 3, 8, 2048)
    cot = cotangent.reshape(16, 3, 8, 2048)
    gain = norm_gain.astype(F32).reshape(1, 2048)
    mixed, grad, g_q, g_k, g_v, g_o, gsum = block_call(tok, cot, w_query, w_key, w_value, w_out, gain)
    index = lax.axis_index("dp") * 16 + lax.axis_index("tm")
    grad_gain = lax.dynamic_index_in_dim(gsum.reshape(128, 16), index, 0, keepdims=False)
    shape = (1, 1, 384, 2048)
    return mixed.reshape(shape), grad.reshape(shape), grad_gain, g_q, g_k, g_v, g_o


def solution(mesh):
    rows = P("dp", "tm", None, None)
    weight = P(("dp", "tm"), None)
    return jax.shard_map(
        on_device,
        mesh=mesh,
        in_specs=(rows, rows, P()) + (weight,) * 4,
        out_specs=(rows, rows, P(("dp", "tm"))) + (weight,) * 4,
        check_vma=False,
    )
```

time: 815 us -> 187 us (0.23); the launches traced: 804 us -> 187 us
  waiting for transfers between devices: 470 us -> 0 us
  Pallas kernels: 0 us -> 177 us
  blocking collectives: 126 us -> 0 us
  matrix products: 69.5 us -> 0 us
  local copies, waits for them, and re-layouts: 66.8 us -> 7.82 us
  other arithmetic: 39.8 us -> 1.29 us
  between operations: 17 us -> 0.67 us
  starting transfers between devices: 15 us -> 0 us
    reduce_scatter x7 -> x0, waiting for transfers between devices: 238 us -> none  [the longest x1 73.6 us: on_device(): lax.psum_scatter(partial_sums[2].astype(jnp.bfloat16), 'tm', scatter_dime...]
    pallas_call x0 -> x1, Pallas kernels: none -> 177 us  [block_call(): pl.pallas_call(block_kernel, out_shape=(sds(rows, BF), sds(rows, BF)) + (...]
    all_gather x4 -> x0, waiting for transfers between devices: 168 us -> none  [the longest x1 67.4 us: on_device(): lax.all_gather(w_value, ('dp', 'tm'), axis=0, tiled=True)]
    all_to_all x5 -> x0, blocking collectives: 77.4 us -> none  [the longest x1 19.7 us: on_device(): lax.all_to_all(attended[0], 'tm', split_axis=0, concat_axis=1, tiled=True)]
    dot_general x17 -> x0, matrix products: 65.4 us -> none  [the longest x4 19.4 us: transpose_dot(): lax.dot_general(left, right, (((0,), (0,)), ((), ())), preferred_element_...]
    unnamed x13 -> x0, waiting for transfers between devices: 64.4 us -> none
    unnamed x2 -> x0, blocking collectives: 49 us -> none
    unnamed x54 -> x16, local copies, waits for them, and re-layouts: 40.6 us -> 6.53 us
  transfers between devices with their start and end apart: 15 -> 0, of which waited for: 8 -> 0; matrix products, arithmetic and copies ran while one was open for 21% -> 0% of each run, Pallas kernels for 0% -> 0%
where the time goes in v2:
time: 187 us
  Pallas kernels  177 us (95%)
  local copies, waits for them, and re-layouts  7.82 us (4%)
    pallas_call x1, Pallas kernels, block_call(): pl.pallas_call(block_kernel, out_shape=(sds(rows, BF), sds(rows, BF)) + (...  177 us
    unnamed x16, local copies, waits for them, and re-layouts  6.53 us

profile of v2, /device:TPU:1, one launch (start us, length us, event | category | flops | bytes accessed | tf_op | source)
XLA Modules:
  0.0 186.7 jit_solution(14531184618141454822)
XLA Ops:
  0.6 1.3 reshape.41
  1.9 176.9 %block.1 = (bf16[16,3,8,2048]{3,2,1,0:T(8,128)(2,1)}, bf16[16,3,8,2048]{3,2,1,0:T(8,128)(2,1)}, f32[16,1024]{1,0:T(8,128)}, f32[16,1024]{1,0:T(8,128)}, f32[16,1...) custom-call(bf16[16,3,8,2048]{3,2,1,0:T(8,128)(2,1)} %bitcast.7, bf16[16,3,8,2048]{3,2,1,0:T(8,128)(2,1)} %bitcast.8, ...), custom_call_target="tpu_custom_call" | custom-call | tf_op jit(solution)/shard_map/block/pallas_call | solution.py:526
  178.8 0.8 reshape.40
  179.6 0.5 dynamic-slice_bitcast_fusion
  180.1 0.0 copy-start
  180.1 2.8 %copy.20 = bf16[1,1,384,2048]{3,2,1,0:T(8,128)(2,1)} copy(bf16[1,1,384,2048]{3,2,1,0:T(8,128)(2,1)} %bitcast.10) | data formatting | bytes 3145728
  183.0 0.0 copy-done
  183.0 0.0 copy-start.4
  183.0 0.0 copy-start.3
  183.0 0.0 copy-start.2
  183.0 0.0 copy-start.1
  183.0 1.1 copy.21
  184.1 0.0 copy-done.4
  184.1 0.6 copy.22
  184.8 0.0 copy-done.3
  184.8 0.6 copy.23
  185.4 0.0 copy-done.2
  185.4 0.6 copy.24
  186.0 0.0 copy-done.1
  186.0 0.6 copy.25
Async XLA Ops:
  180.1 2.9 %copy-start = (bf16[16,3,8,2048]{3,2,1,0:T(8,128)(2,1)S(1)}, bf16[16,3,8,2048]{3,2,1,0:T(8,128)(2,1)}, u32[]{:S(2)}) copy-start(bf16[16,3,8,2048]{3,2,1,0:T(8,128)(2,1)} %get-tuple-element.15) | copy-start | bytes 4718596
  183.0 1.2 copy-start.4
  183.0 1.8 copy-start.3
  183.0 2.4 %copy-start.2 = (f32[16,1024]{1,0:T(8,128)S(1)}, f32[16,1024]{1,0:T(8,128)}, u32[]{:S(2)}) copy-start(f32[16,1024]{1,0:T(8,128)} %get-tuple-element.33) | copy-start | bytes 196612
  183.0 3.1 %copy-start.1 = (f32[8,2048]{1,0:T(8,128)S(1)}, f32[8,2048]{1,0:T(8,128)}, u32[]{:S(2)}) copy-start(f32[8,2048]{1,0:T(8,128)} %get-tuple-element.34) | copy-start | bytes 196612

commit v3 on v2

--- a/solution.py
+++ b/solution.py
@@ -8,6 +8,7 @@
 from jax.sharding import PartitionSpec as P
 
 MESH = pl.DeviceIdType.MESH
+CUT = 1024
 VMEM_LIMIT = 62 * 1024 * 1024
 
 
@@ -82,6 +83,24 @@
             copy.wait_send()
 
 
+class Direct:
+    def __init__(self, block, place, p, sems, first):
+        b = block(p)
+        self.copies = [rcopy(b, b, sems, first + d - 1, place(up(p, d))) for d in (1, 2, 3)]
+
+    def start(self):
+        for copy in self.copies:
+            copy.start()
+
+    def arrive(self):
+        for copy in self.copies:
+            copy.wait_recv()
+
+    def finish(self):
+        for copy in self.copies:
+            copy.wait_send()
+
+
 def nt(a, b):
     return lax.dot_general(a, b, (((1,), (1,)), ((), ())), preferred_element_type=jnp.float32)
 
@@ -97,6 +116,34 @@
 FACTOR = 128 ** (-0.5)
 BF = jnp.bfloat16
 F32 = jnp.float32
+
+
+def add(out, terms):
+    @pl.loop(0, out.shape[0])
+    def _(i):
+        value = terms[0][i].astype(F32)
+        for term in terms[1:]:
+            value = value + term[i].astype(F32)
+        out[i] = value.astype(out.dtype)
+
+
+class DirectSum:
+    def __init__(self, part, place, p, sems, first, land, total):
+        self.own, self.land, self.total = part(p), land, total
+        self.copies = [rcopy(part(up(p, d)), land.at[d - 1], sems, first + d - 1, place(up(p, d))) for d in (1, 2, 3)]
+
+    def start(self):
+        for copy in self.copies:
+            copy.start()
+
+    def finish(self):
+        for copy in self.copies:
+            copy.wait_recv()
+        add(self.total, [self.own] + [self.land.at[d] for d in range(3)])
+
+    def drain(self):
+        for copy in self.copies:
+            copy.wait_send()
 
 
 class RingSum:
@@ -116,30 +163,20 @@
         self.d = self.copy(2, self.part(up(p, 1), 1), self.land.at[0, 1], 1)
         self.e = self.copy(3, self.part(up(p, 3), 0), self.land.at[1, 0], 3)
 
-    def add(self, out, terms):
-        lead = out.shape[0]
-
-        @pl.loop(0, lead)
-        def _(i):
-            value = terms[0][i].astype(F32)
-            for term in terms[1:]:
-                value = value + term[i].astype(F32)
-            out[i] = value.astype(out.dtype)
-
     def relay(self):
         p = self.p
         self.a.wait_recv()
-        self.add(self.via.at[2], [self.via.at[0], self.part(up(p, 1), 0)])
+        add(self.via.at[2], [self.via.at[0], self.part(up(p, 1), 0)])
         self.f = self.copy(4, self.via.at[2], self.land.at[0, 0], 1)
         self.b.wait_recv()
-        self.add(self.via.at[3], [self.via.at[1], self.part(up(p, 3), 1)])
+        add(self.via.at[3], [self.via.at[1], self.part(up(p, 3), 1)])
         self.g = self.copy(5, self.via.at[3], self.land.at[1, 1], 3)
 
     def finish(self):
         for c in (self.d, self.e, self.f, self.g):
             c.wait_recv()
         for h in range(2):
-            self.add(self.total(h), [self.part(self.p, h), self.land.at[0, h], self.land.at[1, h]])
+            add(self.total(h), [self.part(self.p, h), self.land.at[0, h], self.land.at[1, h]])
 
     def drain(self):
         for c in (self.a, self.b, self.d, self.e, self.f, self.g):
@@ -152,8 +189,9 @@
 
 def block_kernel(tok, cot, wq, wk, wv, w_out, gain, mixed, grad, g_q, g_k, g_v, g_o, gsum,
                  t, ct, w, wo, wom, normed, cotm, scaled, proj, back, mask, mp, dp, mr, dr, om, og,
-                 via1, land1, sum1, via2, land2, sum2, via3, land3, p3, p3r,
-                 qvia1, qland1, q1, qvia2, qland2, q2, qvia3, qland3, q3,
+                 via1, land1, sum1, land2, sum2, land3, p3, p3r,
+                 dvia, dland, d1, dland2, d2, dland3, evia, eland, e1, eland2, e2, eland3,
+                 fvia, fland, f1, fland2, f2, fland3, q3,
                  gg, gland, gacc,
                  ag_s, ag_r, w_s, w_r, w_l, in_s, in_r, fw_s, fw_r, sw_s, sw_r, bk_s, bk_r, rs_s, rs_r, gn_s, gn_r, loc):
     y, c, z, x = coords()
@@ -190,30 +228,27 @@
 
     ag = (ag_s, ag_r)
 
-    def yx(i):
-        a = Ring(lambda v: w.at[i, y, :, z, v], lambda v, k: w.at[i, y, k, z, v], at_x, x, ag, 12 * i)
-        b = Ring(lambda v: w.at[i, y, :, v], lambda v, k: w.at[i, y, k, v], at_z, z, ag, 12 * i + 4)
-        d = Ring(lambda v: w.at[i, v], lambda v, k: w.at[i, v, k], at_y, y, ag, 12 * i + 8)
-        return a, b, d
-
-    qa, qb, qc = yx(0)
-    ka, kb, kc = yx(1)
-    va = Ring(lambda v: w.at[2, v, :, z, x], lambda v, k: w.at[2, v, k, z, x], at_y, y, ag, 24)
-    vb = Ring(lambda v: w.at[2, :, :, v, x], lambda v, k: w.at[2, :, k, v, x], at_z, z, ag, 28)
-    vc = Ring(lambda v: w.at[2, :, :, :, v], lambda v, k: w.at[2, :, k, :, v], at_x, x, ag, 32)
-    oa = Ring(lambda v: wo.at[v, z, x], lambda v, k: wo.at[v, z, x, :, pl.ds(1024 * k, 1024)], at_y, y, ag, 36)
-    ob = Ring(lambda v: wo.at[:, z, v], lambda v, k: wo.at[pl.ds(2 * k, 2), z, v], at_x, x, ag, 40)
-    oc = Ring(lambda v: wo.at[:, v], lambda v, k: wo.at[pl.ds(2 * k, 2), v], at_z, z, ag, 44)
-    rings = (qa, qb, qc, ka, kb, kc, va, vb, vc, oa, ob, oc)
-
-    own_o.wait()
-    oa.start()
-    for copy in own_w:
-        copy.wait()
-    for copy in swap_w:
-        copy.wait_recv()
-    for r in (qa, va, ka):
-        r.start()
+    qa = Direct(lambda v: w.at[0, y, :, z, v], at_x, x, ag, 0)
+    qb = Direct(lambda v: w.at[0, y, :, v], at_z, z, ag, 3)
+    qc = Ring(lambda v: w.at[0, v], lambda v, k: w.at[0, v, k], at_y, y, ag, 6)
+    ka = Direct(lambda v: w.at[1, y, :, v, x], at_z, z, ag, 10)
+    kb = Direct(lambda v: w.at[1, v, :, :, x], at_y, y, ag, 13)
+    kc = Ring(lambda v: w.at[1, :, :, :, v], lambda v, k: w.at[1, :, k, :, v], at_x, x, ag, 16)
+    va = Direct(lambda v: w.at[2, v, :, z, x], at_y, y, ag, 20)
+    vb = Direct(lambda v: w.at[2, :, :, z, v], at_x, x, ag, 23)
+    vc = Ring(lambda v: w.at[2, :, :, v], lambda v, k: w.at[2, :, k, v], at_z, z, ag, 26)
+    o0, o1, o2 = (pl.ds(0, CUT), pl.ds(CUT, (2048 - CUT) // 2), pl.ds(CUT + (2048 - CUT) // 2, (2048 - CUT) // 2))
+    da = Direct(lambda v: wo.at[y, v, x, :, o0], at_z, z, ag, 30)
+    db = Direct(lambda v: wo.at[y, :, v, :, o0], at_x, x, ag, 33)
+    dc = Ring(lambda v: wo.at[v, :, :, :, o0], lambda v, k: wo.at[v, pl.ds(2 * k, 2), :, :, o0], at_y, y, ag, 36)
+    ea = Direct(lambda v: wo.at[v, z, x, :, o1], at_y, y, ag, 40)
+    eb = Direct(lambda v: wo.at[:, v, x, :, o1], at_z, z, ag, 43)
+    ec = Ring(lambda v: wo.at[:, :, v, :, o1], lambda v, k: wo.at[pl.ds(2 * k, 2), :, v, :, o1], at_x, x, ag, 46)
+    fa = Direct(lambda v: wo.at[y, z, v, :, o2], at_x, x, ag, 50)
+    fb = Direct(lambda v: wo.at[v, z, :, :, o2], at_y, y, ag, 53)
+    fc = Ring(lambda v: wo.at[:, v, :, :, o2], lambda v, k: wo.at[pl.ds(2 * k, 2), v, :, :, o2], at_z, z, ag, 56)
+    firsts, seconds, thirds = (qa, ka, va, da, ea, fa), (qb, kb, vb, db, eb, fb), (qc, kc, vc, dc, ec, fc)
+    rings = firsts + seconds + thirds
 
     def spread(g):
         for j, (src, staged, dst) in enumerate([(tok, om, t), (cot, og, ct)]):
@@ -247,7 +282,7 @@
             s = centered * inverse
             scaled[pl.ds(pl.multiple_of(i * 32, 32), 32), :] = s
             rows = pl.ds(pl.multiple_of(g * 256 + i * 32, 32), 32)
-            normed[rows, :] = (s * gain[...]).astype(BF)
+            normed[rows, :] = (s * gain[...].astype(F32)).astype(BF)
             cotm[rows, :] = ct[k, g, pl.ds(f, 4)].astype(F32).reshape(32, 2048).astype(BF)
 
     def project(g, i):
@@ -310,7 +345,7 @@
             centered = value - jnp.mean(value, axis=-1, keepdims=True)
             inverse = lax.rsqrt(jnp.mean(centered * centered, axis=-1, keepdims=True) + 1e-05)
             s = centered * inverse
-            ds = (dp[g, c, fs].astype(F32) + dr[g, fs].astype(F32)) * gain[...].reshape(1, 1, 2048)
+            ds = (dp[g, c, fs].astype(F32) + dr[g, fs].astype(F32)) * gain[...].astype(F32).reshape(1, 1, 2048)
             first = jnp.mean(ds, axis=-1, keepdims=True)
             second = jnp.mean(ds * s, axis=-1, keepdims=True)
             og[g, fs] = (inverse * (ds - first - s * second) + ct[c, g, fs].astype(F32)).astype(BF)
@@ -336,27 +371,30 @@
 
     rs = (rs_s, rs_r)
 
-    def sums(i):
-        if i < 2:
-            a = RingSum(lambda v, h: w.at[i, v, h], at_y, y, rs, 18 * i, via1.at[i], land1.at[i], lambda h: sum1.at[i, h])
-            b = RingSum(lambda v, h: sum1.at[i, h, v], at_z, z, rs, 18 * i + 6, via2.at[i], land2.at[i], lambda h: sum2.at[i, h])
-            d = RingSum(lambda v, h: sum2.at[i, h, pl.ds(v, 1)], at_x, x, rs, 18 * i + 12, via3.at[i], land3.at[i],
-                        lambda h: p3.at[i, pl.ds(h, 1)])
-        else:
-            a = RingSum(lambda v, h: w.at[i, :, h, :, v], at_x, x, rs, 18 * i, via1.at[i], land1.at[i], lambda h: sum1.at[i, h])
-            b = RingSum(lambda v, h: sum1.at[i, h, :, v], at_z, z, rs, 18 * i + 6, via2.at[i], land2.at[i], lambda h: sum2.at[i, h])
-            d = RingSum(lambda v, h: sum2.at[i, h, pl.ds(v, 1)], at_y, y, rs, 18 * i + 12, via3.at[i], land3.at[i],
-                        lambda h: p3.at[i, pl.ds(h, 1)])
-        return a, b, d
-
-    qx, qy, qz = sums(0)
-    kx, ky, kz = sums(1)
-    vx, vy, vz = sums(2)
-    ox = RingSum(lambda v, h: wo.at[pl.ds(2 * h, 2), v], at_z, z, rs, 54, qvia1, qland1, lambda h: q1.at[pl.ds(2 * h, 2)])
-    oy = RingSum(lambda v, h: q1.at[pl.ds(2 * h, 2), v], at_x, x, rs, 60, qvia2, qland2, lambda h: q2.at[pl.ds(2 * h, 2)])
-    oz = RingSum(lambda v, h: q2.at[pl.ds(v, 1), :, pl.ds(1024 * h, 1024)], at_y, y, rs, 66, qvia3, qland3,
-                 lambda h: q3.at[:, :, pl.ds(1024 * h, 1024)])
-    all_sums = (qx, qy, qz, kx, ky, kz, vx, vy, vz, ox, oy, oz)
+    def term_ring(i, part, place, p):
+        return RingSum(part, place, p, rs, 12 * i, via1.at[i], land1.at[i], lambda h: sum1.at[i, h])
+
+    def term_sums(i, part2, place2, p2, place3, p3_):
+        second = DirectSum(part2, place2, p2, rs, 12 * i + 6, land2.at[i], sum2.at[i])
+        third = DirectSum(lambda v: sum2.at[i, :, v], place3, p3_, rs, 12 * i + 9, land3.at[i], p3.at[i])
+        return second, third
+
+    qx = term_ring(0, lambda v, h: w.at[0, v, h], at_y, y)
+    qy, qz = term_sums(0, lambda v: sum1.at[0, :, v], at_z, z, at_x, x)
+    kx = term_ring(1, lambda v, h: w.at[1, :, h, :, v], at_x, x)
+    ky, kz = term_sums(1, lambda v: sum1.at[1, :, v], at_y, y, at_z, z)
+    vx = term_ring(2, lambda v, h: w.at[2, :, h, v], at_z, z)
+    vy, vz = term_sums(2, lambda v: sum1.at[2, :, :, v], at_x, x, at_y, y)
+    dx = RingSum(lambda v, h: wo.at[v, pl.ds(2 * h, 2), :, :, o0], at_y, y, rs, 36, dvia, dland, lambda h: d1.at[pl.ds(2 * h, 2)])
+    dy = DirectSum(lambda v: d1.at[:, v], at_x, x, rs, 42, dland2, d2)
+    dz = DirectSum(lambda v: d2.at[pl.ds(v, 1)], at_z, z, rs, 45, dland3, q3.at[:, :, o0])
+    ex = RingSum(lambda v, h: wo.at[pl.ds(2 * h, 2), :, v, :, o1], at_x, x, rs, 48, evia, eland, lambda h: e1.at[pl.ds(2 * h, 2)])
+    ey = DirectSum(lambda v: e1.at[:, v], at_z, z, rs, 54, eland2, e2)
+    ez = DirectSum(lambda v: e2.at[pl.ds(v, 1)], at_y, y, rs, 57, eland3, q3.at[:, :, o1])
+    fx = RingSum(lambda v, h: wo.at[pl.ds(2 * h, 2), v, :, :, o2], at_z, z, rs, 60, fvia, fland, lambda h: f1.at[pl.ds(2 * h, 2)])
+    fy = DirectSum(lambda v: f1.at[v], at_y, y, rs, 66, fland2, f2)
+    fz = DirectSum(lambda v: f2.at[pl.ds(v, 1)], at_x, x, rs, 69, fland3, q3.at[:, :, o2])
+    all_sums = (qx, qy, qz, kx, ky, kz, vx, vy, vz, dx, dy, dz, ex, ey, ez, fx, fy, fz)
 
     def gain_start(k, src):
         place, p = [(at_y, y), (at_z, z), (at_x, x)][k]
@@ -372,34 +410,38 @@
             copy.wait_recv()
         gacc[k] = src[...] + gland[3 * k] + gland[3 * k + 1] + gland[3 * k + 2]
 
-    spread(0)
+    own_o.wait()
+    for r in (da, ea, fa):
+        r.start()
+    for copy in own_w:
+        copy.wait()
+    for copy in swap_w:
+        copy.wait_recv()
+    for r in (qa, ka, va):
+        r.start()
     rows_i = lax.broadcasted_iota(jnp.int32, (128, 128), 0)
     cols_i = lax.broadcasted_iota(jnp.int32, (128, 128), 1)
     same = lax.rem(rows_i + 128 - cols_i, 8) == 0
     mask[...] = jnp.where(same & (cols_i <= rows_i), 0.0, -1e30)
-    for r in (qa, oa, va, ka):
-        r.relay()
-    for a, b in ((qa, qb), (oa, ob), (va, vb), (ka, kb)):
+    for a, b in zip(firsts, seconds):
         a.arrive()
         b.start()
-    for r in (qb, ob, vb, kb):
-        r.relay()
-    for a, b in ((qb, qc), (ob, oc), (vb, vc), (kb, kc)):
+    for a, b in zip(seconds, thirds):
         a.arrive()
         b.start()
+    spread(0)
+    for r in thirds:
+        r.relay()
+    spread(1)
     pass_on(0)
     norm(0)
-    qc.relay()
-    vc.relay()
-    oc.relay()
-    spread(1)
-    kc.relay()
-    spread(2)
     qc.arrive()
     project(0, 0)
     vc.arrive()
     project(0, 2)
-    oc.arrive()
+    spread(2)
+    for r in (dc, ec, fc):
+        r.arrive()
 
     @pl.loop(0, 4)
     def _(j):
@@ -429,44 +471,36 @@
     g0 = gain_start(0, gland.at[9])
     for r in rings:
         r.finish()
+    o_terms()
+    for r in (dx, ex, fx):
+        r.start()
+    w_terms(0)
+    qx.start()
     w_terms(1)
     kx.start()
+    finalize(2)
     w_terms(2)
     vx.start()
-    finalize(2)
-    o_terms()
-    ox.start()
+    for r in (dx, ex, fx):
+        r.relay()
+    qx.relay()
     kx.relay()
-    w_terms(0)
-    qx.start()
-    vx.relay()
-    ox.relay()
     gain_finish(0, gland.at[9], g0)
     g1 = gain_start(1, gacc.at[0])
-    kx.finish()
-    ky.start()
-    qx.relay()
+    vx.relay()
+    for a, b in ((dx, dy), (ex, ey), (fx, fy)):
+        a.finish()
+        b.start()
+    for a, b in ((qx, qy), (kx, ky)):
+        a.finish()
+        b.start()
+    gain_finish(1, gacc.at[0], g1)
+    g2 = gain_start(2, gacc.at[1])
     vx.finish()
     vy.start()
-    ox.finish()
-    oy.start()
-    ky.relay()
-    gain_finish(1, gacc.at[0], g1)
-    g2 = gain_start(2, gacc.at[1])
-    vy.relay()
-    oy.relay()
-    ky.finish()
-    kz.start()
-    qx.finish()
-    qy.start()
-    vy.finish()
-    vz.start()
-    oy.finish()
-    oz.start()
-    kz.relay()
-    vz.relay()
-    oz.relay()
-    qy.relay()
+    for a, b in ((dy, dz), (ey, ez), (fy, fz), (qy, qz), (ky, kz), (vy, vz)):
+        a.finish()
+        b.start()
     gain_finish(2, gacc.at[1], g2)
     g3 = rcopy(gacc.at[2], gland.at[10], (gn_s, gn_r), 9, sib)
     g3.start()
@@ -484,22 +518,17 @@
             out[:, pl.ds(pl.multiple_of((2 * j + c) * 128, 128), 128)] = p3[i, c, :, cols]
             out[:, pl.ds(pl.multiple_of((2 * j + 1 - c) * 128, 128), 128)] = p3r[i, :, cols]
 
-    kz.finish()
-    across(1)
-    qy.finish()
-    qz.start()
-    vz.finish()
-    across(2)
-    oz.finish()
+    for r in (dz, ez, fz):
+        r.finish()
+    for i, r in enumerate((qz, kz, vz)):
+        r.finish()
+        across(i)
     g_o[...] = q3[0]
-    put(1, g_k)
-    qz.relay()
-    put(2, g_v)
     g3.wait_recv()
     gsum[...] = gacc[2] + gland[10]
-    qz.finish()
-    across(0)
     put(0, g_q)
+    put(1, g_k)
+    put(2, g_v)
     for j, (src, dst) in enumerate([(om, mixed), (og, grad)]):
         wait_bytes(dst, bk_r.at[j])
         wait_bytes(src.at[:, pl.ds(0, 15)], bk_s.at[j])
@@ -522,7 +551,10 @@
     def ring(lead, unit):
         return [V(lead + (4,) + unit, BF), V(lead + (2, 2) + unit, BF)]
 
-    sems = [48, 48, 12, 12, 12, 6, 6, 6, 6, 9, 9, 2, 2, 72, 72, 10, 10, 7]
+    def out_sums(n):
+        return ring((), (2, 4, 8, n)) + [V(u, BF) for u in ((4, 4, 8, n), (3, 4, 8, n), (4, 8, n), (3, 1, 8, n))]
+
+    sems = [60, 60, 12, 12, 12, 6, 6, 6, 6, 9, 9, 2, 2, 72, 72, 10, 10, 7]
     return pl.pallas_call(
         block_kernel,
         out_shape=(sds(rows, BF), sds(rows, BF))
@@ -538,15 +570,13 @@
         + [V(groups, BF)] * 4
         + ring((3,), (4, 4, 16, 512))
         + [V((3, 2, 4, 4, 16, 512), BF)]
-        + ring((3,), (4, 16, 512))
+        + [V((3, 3, 2, 4, 16, 512), BF)]
         + [V((3, 2, 4, 16, 512), BF)]
-        + ring((3,), (1, 16, 512))
+        + [V((3, 3, 2, 16, 512), BF)]
         + [V((3, 2, 16, 512), F32), V((3, 16, 512), F32)]
-        + ring((), (2, 4, 8, 2048))
-        + [V((4, 4, 8, 2048), BF)]
-        + ring((), (2, 8, 2048))
-        + [V((4, 8, 2048), BF)]
-        + ring((), (1, 8, 1024))
+        + out_sums(CUT)
+        + out_sums((2048 - CUT) // 2)
+        + out_sums((2048 - CUT) // 2)
         + [V((1, 8, 2048), F32)]
         + [V((1, 2048), F32), V((11, 16, 128), F32), V((3, 16, 128), F32)]
         + [sem((n,)) for n in sems],
@@ -555,15 +585,47 @@
     )(tok, cot, wq, wk, wv, w_out, gain)
 
 
+def finish_kernel(*refs):
+    ins, outs, gsum, gain_out, held, sems = refs[:6], refs[7:13], refs[6], refs[13], refs[14:20], refs[20]
+    pieces = [(i, pl.ds(4 * k, 4)) for i in range(2) for k in range(4)] + [(i, slice(None)) for i in range(2, 6)]
+    enter = [pltpu.make_async_copy(ins[i].at[at], held[i].at[at], sems.at[n]) for n, (i, at) in enumerate(pieces)]
+    leave = [pltpu.make_async_copy(held[i].at[at], outs[i].at[at], sems.at[12 + n]) for n, (i, at) in enumerate(pieces)]
+    for copy in enter:
+        copy.start()
+    index = lax.axis_index("dp") * 16 + lax.axis_index("tm")
+    row = gsum[pl.ds(lax.div(index, 8), 1), :]
+    out = jnp.zeros((1, 16), F32)
+    for i in range(8):
+        out = jnp.where(lax.rem(index, 8) == i, row[:, 16 * i : 16 * i + 16], out)
+    gain_out[...] = out
+    for before, after in zip(enter, leave):
+        before.wait()
+        after.start()
+    for copy in leave:
+        copy.wait()
+
+
+def finish_call(arrays, gsum):
+    vm = pl.BlockSpec(memory_space=pltpu.VMEM)
+    any_ = pl.BlockSpec(memory_space=pl.ANY)
+    return pl.pallas_call(
+        finish_kernel,
+        out_shape=tuple(jax.ShapeDtypeStruct(a.shape, a.dtype) for a in arrays) + (jax.ShapeDtypeStruct((1, 16), F32),),
+        in_specs=[any_] * 6 + [vm],
+        out_specs=(any_,) * 6 + (vm,),
+        scratch_shapes=[pltpu.VMEM(a.shape, a.dtype) for a in arrays] + [pltpu.SemaphoreType.DMA((24,))],
+        name="finish",
+    )(*arrays, gsum)
+
+
 def on_device(tokens, cotangent, norm_gain, w_query, w_key, w_value, w_out):
     tok = tokens.reshape(16, 3, 8, 2048)
     cot = cotangent.reshape(16, 3, 8, 2048)
-    gain = norm_gain.astype(F32).reshape(1, 2048)
-    mixed, grad, g_q, g_k, g_v, g_o, gsum = block_call(tok, cot, w_query, w_key, w_value, w_out, gain)
-    index = lax.axis_index("dp") * 16 + lax.axis_index("tm")
-    grad_gain = lax.dynamic_index_in_dim(gsum.reshape(128, 16), index, 0, keepdims=False)
+    gain = norm_gain.reshape(1, 2048)
+    *arrays, gsum = block_call(tok, cot, w_query, w_key, w_value, w_out, gain)
+    mixed, grad, g_q, g_k, g_v, g_o, grad_gain = finish_call(arrays, gsum)
     shape = (1, 1, 384, 2048)
-    return mixed.reshape(shape), grad.reshape(shape), grad_gain, g_q, g_k, g_v, g_o
+    return mixed.reshape(shape), grad.reshape(shape), grad_gain.reshape(16), g_q, g_k, g_v, g_o
 
 
 def solution(mesh):

time: 187 us -> 170 us (0.909)
  Pallas kernels: 177 us -> 167 us
  local copies, waits for them, and re-layouts: 7.82 us -> 1.29 us
    pallas_call x1, Pallas kernels: 177 us -> 163 us  [block_call(): pl.pallas_call(block_kernel, out_shape=(sds(rows, BF), sds(rows, BF)) + (...]
    unnamed x16 -> x0, local copies, waits for them, and re-layouts: 6.53 us -> none
    pallas_call x0 -> x1, Pallas kernels: none -> 4.15 us  [finish_call(): pl.pallas_call(finish_kernel, out_shape=tuple((jax.ShapeDtypeStruct(a.sha...]
where the time goes in v3:
time: 170 us; the launch traced here: 169 us
  Pallas kernels  167 us (98%)
    pallas_call x1, Pallas kernels, block_call(): pl.pallas_call(block_kernel, out_shape=(sds(rows, BF), sds(rows, BF)) + (...  163 us
    pallas_call x1, Pallas kernels, finish_call(): pl.pallas_call(finish_kernel, out_shape=tuple((jax.ShapeDtypeStruct(a.sha...  4.15 us

profile of v3, /device:TPU:1, one launch (start us, length us, event | category | flops | bytes accessed | tf_op | source)
XLA Modules:
  0.0 169.5 jit_solution(17039802375480894342)
XLA Ops:
  0.6 1.3 reshape.34.gain
  1.9 163.2 %block.1 = (bf16[16,3,8,2048]{3,2,1,0:T(8,128)(2,1)}, bf16[16,3,8,2048]{3,2,1,0:T(8,128)(2,1)}, f32[16,1024]{1,0:T(8,128)}, f32[16,1024]{1,0:T(8,128)}, f32[16,1...) custom-call(bf16[16,3,8,2048]{3,2,1,0:T(8,128)(2,1)} %bitcast.5, bf16[16,3,8,2048]{3,2,1,0:T(8,128)(2,1)} %bitcast.6, ...), custom_call_target="tpu_custom_call" | custom-call | tf_op jit(solution)/shard_map/block/pallas_call | solution.py:558
  165.1 4.1 %finish.1 = (bf16[16,3,8,2048]{3,2,1,0:T(8,128)(2,1)}, bf16[16,3,8,2048]{3,2,1,0:T(8,128)(2,1)}, f32[16,1024]{1,0:T(8,128)}, f32[16,1024]{1,0:T(8,128)}, f32[16,...) custom-call(bf16[16,3,8,2048]{3,2,1,0:T(8,128)(2,1)} %get-tuple-element.21.refs_0_, ...), custom_call_target="tpu_custom_call" | custom-call | tf_op jit(solution)/shard_map/finish/pallas_call | solution.py:611

commit v4 on v3

--- a/solution.py
+++ b/solution.py
@@ -188,25 +188,27 @@
 
 
 def block_kernel(tok, cot, wq, wk, wv, w_out, gain, mixed, grad, g_q, g_k, g_v, g_o, gsum,
-                 t, ct, w, wo, wom, normed, cotm, scaled, proj, back, mask, mp, dp, mr, dr, om, og,
+                 t, cth, w, wo, wom, normed, cotm, scaled, proj, ups, upt, back, atts, atth, attm, mask,
+                 mrh, dp, dr, om, og, gh,
                  via1, land1, sum1, land2, sum2, land3, p3, p3r,
                  dvia, dland, d1, dland2, d2, dland3, evia, eland, e1, eland2, e2, eland3,
                  fvia, fland, f1, fland2, f2, fland3, q3,
                  gg, gland, gacc,
-                 ag_s, ag_r, w_s, w_r, w_l, in_s, in_r, fw_s, fw_r, sw_s, sw_r, bk_s, bk_r, rs_s, rs_r, gn_s, gn_r, loc):
+                 ag_s, ag_r, w_s, w_r, w_l, in_s, in_r, fw_s, fw_r, c_s, c_r, up_s, up_r, at_s, at_r, sw_s, sw_r,
+                 bk_s, bk_r, rs_s, rs_r, gn_s, gn_r, loc, out_l):
     y, c, z, x = coords()
     tm = z * 4 + x
     sib = device(y, 1 - c, z, x)
     at_x = lambda v: device(y, c, z, v)
     at_y = lambda v: device(v, c, z, x)
     at_z = lambda v: device(y, c, v, x)
-
-    stage = []
-    for j, (src, dst) in enumerate([(tok, om), (cot, og)]):
-        for g in range(3):
-            copy = pltpu.make_async_copy(src.at[:, g], dst.at[g], loc.at[3 * j + g])
-            copy.start()
-            stage.append(copy)
+    mph = cth
+
+    stage, cot_own = [], []
+    for g in range(3):
+        copy = pltpu.make_async_copy(tok.at[:, g], om.at[g], loc.at[g])
+        copy.start()
+        stage.append(copy)
     own_o = pltpu.make_async_copy(w_out, wo.at[y, z, x], loc.at[6])
     own_o.start()
     own_w = []
@@ -216,6 +218,10 @@
             copy = pltpu.make_async_copy(src.at[:, cols], w.at[i, y, c, z, x, :, pl.ds(128 * j, 128)], w_l.at[4 * i + j])
             copy.start()
             own_w.append(copy)
+    for g in range(3):
+        copy = pltpu.make_async_copy(cot.at[:, g], cth.at[g, c], loc.at[3 + g])
+        copy.start()
+        cot_own.append(copy)
     greet(y, c, z, x)
 
     swap_w = []
@@ -225,9 +231,14 @@
             copy = rcopy(src.at[:, cols], w.at[i, y, c, z, x, :, pl.ds(128 * j, 128)], (w_s, w_r), 4 * i + j, sib)
             copy.start()
             swap_w.append(copy)
+    swap_c = []
+    for g in range(3):
+        cot_own[g].wait()
+        copy = rcopy(cth.at[g, c], cth.at[g, c], (c_s, c_r), g, sib)
+        copy.start()
+        swap_c.append(copy)
 
     ag = (ag_s, ag_r)
-
     qa = Direct(lambda v: w.at[0, y, :, z, v], at_x, x, ag, 0)
     qb = Direct(lambda v: w.at[0, y, :, v], at_z, z, ag, 3)
     qc = Ring(lambda v: w.at[0, v], lambda v, k: w.at[0, v, k], at_y, y, ag, 6)
@@ -250,28 +261,49 @@
     firsts, seconds, thirds = (qa, ka, va, da, ea, fa), (qb, kb, vb, db, eb, fb), (qc, kc, vc, dc, ec, fc)
     rings = firsts + seconds + thirds
 
-    def spread(g):
-        for j, (src, staged, dst) in enumerate([(tok, om, t), (cot, og, ct)]):
-            stage[3 * j + g].wait()
-            pltpu.make_async_copy(src.at[tm, g], dst.at[c, g, tm], in_r.at[2 * g + j]).start()
+    def to_all(send):
         for dz, dx in OFFSETS:
             zz, xx = up(z, dz), up(x, dx)
-            for j, (staged, dst) in enumerate([(om, t), (og, ct)]):
-                rcopy(staged.at[g, zz * 4 + xx], dst.at[c, g, tm], (in_s, in_r), 2 * g + j, device(y, c, zz, xx)).start()
+            send(zz * 4 + xx, device(y, c, zz, xx))
+
+    def spread(g):
+        stage[g].wait()
+        pltpu.make_async_copy(tok.at[tm, g], t.at[c, g, tm], in_r.at[g]).start()
+        to_all(lambda j, place: rcopy(om.at[g, j], t.at[c, g, tm], (in_s, in_r), g, place).start())
 
     passed = {}
 
     def pass_on(g):
-        passed[g] = []
-        for j, dst in enumerate((t, ct)):
-            wait_bytes(dst.at[c, g], in_r.at[2 * g + j])
-            copy = rcopy(dst.at[c, g], dst.at[c, g], (fw_s, fw_r), 2 * g + j, sib)
-            copy.start()
-            passed[g].append(copy)
+        wait_bytes(t.at[c, g], in_r.at[g])
+        passed[g] = rcopy(t.at[c, g], t.at[c, g], (fw_s, fw_r), g, sib)
+        passed[g].start()
+
+    def cot_rows():
+        for g in range(3):
+            swap_c[g].wait_recv()
+
+            @pl.loop(0, 8)
+            def _(i):
+                k, f = lax.div(i, 4), lax.rem(i, 4) * 4
+                rows = pl.ds(pl.multiple_of(g * 256 + i * 32, 32), 32)
+                cotm[rows, :] = cth[g, k, pl.ds(f, 4)].astype(F32).reshape(32, 2048).astype(BF)
+
+    def wo_rows():
+        @pl.loop(0, 4)
+        def _(j):
+            wom[pl.ds(pl.multiple_of(j * 128, 128), 128), :] = wo[j].astype(F32).reshape(128, 2048).astype(BF)
+
+    def upstream():
+        @pl.loop(0, 3)
+        def _(g):
+            rows = pl.ds(pl.multiple_of(g * 256, 256), 256)
+            ups[g] = nt(cotm[rows, :], wom[...]).reshape(2, 16, 8, 512).astype(BF)
+
+        pltpu.make_async_copy(ups.at[:, :, tm], upt.at[:, :, tm], up_r.at[0]).start()
+        to_all(lambda j, place: rcopy(ups.at[:, :, j], upt.at[:, :, tm], (up_s, up_r), 0, place).start())
 
     def norm(g):
-        for copy in passed[g]:
-            copy.wait_recv()
+        passed[g].wait_recv()
 
         @pl.loop(0, 8)
         def _(i):
@@ -283,14 +315,13 @@
             scaled[pl.ds(pl.multiple_of(i * 32, 32), 32), :] = s
             rows = pl.ds(pl.multiple_of(g * 256 + i * 32, 32), 32)
             normed[rows, :] = (s * gain[...].astype(F32)).astype(BF)
-            cotm[rows, :] = ct[k, g, pl.ds(f, 4)].astype(F32).reshape(32, 2048).astype(BF)
 
     def project(g, i):
         rows = pl.ds(g * 256, 256)
         if i < 3:
             proj[i] = nn(normed[rows, :], w[i].reshape(2048, 512)).astype(BF)
         else:
-            proj[3] = nt(cotm[rows, :], wom[...]).astype(BF)
+            proj[3] = upt[g].astype(F32).reshape(256, 512).astype(BF)
 
     def attention(g):
         @pl.loop(0, 4)
@@ -304,20 +335,22 @@
                 e = jnp.exp(s - jnp.max(s, axis=-1, keepdims=True))
                 p = e / jnp.sum(e, axis=-1, keepdims=True)
                 p_b = p.astype(BF)
-                back[3, out, cols] = nn(p_b, v).astype(BF)
+                atts[g, clip, :, :, cols] = nn(p_b, v).reshape(16, 8, 128).astype(BF)
                 d = nt(u, v)
                 ds = (p * (d - jnp.sum(p * d, axis=-1, keepdims=True))).astype(BF)
                 back[0, out, cols] = (nn(ds, k) * FACTOR).astype(BF)
                 back[1, out, cols] = (tn(ds, q) * FACTOR).astype(BF)
                 back[2, out, cols] = tn(p_b, u).astype(BF)
 
+        pltpu.make_async_copy(atts.at[g, :, tm], atth.at[g, :, tm], at_r.at[g]).start()
+        to_all(lambda f, place: rcopy(atts.at[g, :, f], atth.at[g, :, tm], (at_s, at_r), g, place).start())
+
     swapped = {}
 
     def partials(g):
         rows = pl.ds(g * 256, 256)
         for h in range(2):
             half = pl.ds(h * 1024, 1024)
-            mp[g, :, :, :, half] = nn(back[3, rows, :], wom[:, half]).reshape(2, 16, 8, 1024).astype(BF)
             dn = None
             for i in range(3):
                 term = nt(back[i, rows, :], w[i, pl.ds(2 * h, 2)].reshape(1024, 512))
@@ -325,37 +358,67 @@
             dp[g, :, :, :, half] = dn.reshape(2, 16, 8, 1024).astype(BF)
             total = jnp.sum(dn * scaled[:, half], axis=0, keepdims=True)
             gg[:, half] = total if g == 0 else gg[:, half] + total
-        swapped[g] = []
-        for j, (src, dst) in enumerate([(mp, mr), (dp, dr)]):
-            copy = rcopy(src.at[g, 1 - c], dst.at[g], (sw_s, sw_r), 2 * g + j, sib)
-            copy.start()
-            swapped[g].append(copy)
+        swapped[g] = rcopy(dp.at[g, 1 - c], dr.at[g], (sw_s, sw_r), g, sib)
+        swapped[g].start()
 
     def finalize(g):
-        for j, staged in enumerate((om, og)):
-            wait_bytes(staged.at[g, pl.ds(0, 15)], in_s.at[2 * g + j])
-        for copy in swapped[g]:
-            copy.wait_recv()
+        swapped[g].wait_recv()
 
         @pl.loop(0, 4)
         def _(i):
             fs = pl.ds(i * 4, 4)
             value = t[c, g, fs].astype(F32)
-            om[g, fs] = (value + (mp[g, c, fs].astype(F32) + mr[g, fs].astype(F32))).astype(BF)
             centered = value - jnp.mean(value, axis=-1, keepdims=True)
             inverse = lax.rsqrt(jnp.mean(centered * centered, axis=-1, keepdims=True) + 1e-05)
             s = centered * inverse
             ds = (dp[g, c, fs].astype(F32) + dr[g, fs].astype(F32)) * gain[...].astype(F32).reshape(1, 1, 2048)
             first = jnp.mean(ds, axis=-1, keepdims=True)
             second = jnp.mean(ds * s, axis=-1, keepdims=True)
-            og[g, fs] = (inverse * (ds - first - s * second) + ct[c, g, fs].astype(F32)).astype(BF)
-
-        for dz, dx in OFFSETS:
-            zz, xx = up(z, dz), up(x, dx)
-            for j, (src, dst) in enumerate([(om, mixed), (og, grad)]):
-                rcopy(src.at[g, zz * 4 + xx], dst.at[tm, g], (bk_s, bk_r), j, device(y, c, zz, xx)).start()
-        for j, (src, dst) in enumerate([(om, mixed), (og, grad)]):
-            pltpu.make_async_copy(src.at[g, tm], dst.at[tm, g], bk_r.at[j]).start()
+            og[g, fs] = (inverse * (ds - first - s * second)).astype(BF)
+
+        pltpu.make_async_copy(og.at[g, tm], gh.at[g, tm], bk_r.at[g]).start()
+        to_all(lambda f, place: rcopy(og.at[g, f], gh.at[g, tm], (bk_s, bk_r), g, place).start())
+
+    mixed_swap, written = {}, []
+
+    def home_rows(g):
+        wait_bytes(atth.at[g], at_r.at[g])
+        attm[pl.ds(g * 256, 256), :] = atth[g].astype(F32).reshape(256, 512).astype(BF)
+
+    def home(g):
+        rows = pl.ds(g * 256, 256)
+        for h in range(2):
+            half = pl.ds(h * 1024, 1024)
+            mph[g, :, :, :, half] = nn(attm[rows, :], wom[:, half]).reshape(2, 16, 8, 1024).astype(BF)
+        mixed_swap[g] = rcopy(mph.at[g, 1 - c], mrh.at[g], (sw_s, sw_r), 3 + g, sib)
+        mixed_swap[g].start()
+
+    def write(g, j, src, dst):
+        copy = pltpu.make_async_copy(src.at[g], dst.at[:, g], out_l.at[2 * g + j])
+        copy.start()
+        written.append(copy)
+
+    def mixed_out(g):
+        wait_bytes(om.at[g, pl.ds(0, 15)], in_s.at[g])
+        mixed_swap[g].wait_recv()
+
+        @pl.loop(0, 4)
+        def _(i):
+            js = pl.ds(i * 4, 4)
+            om[g, js] = (om[g, js].astype(F32) + (mph[g, c, js].astype(F32) + mrh[g, js].astype(F32))).astype(BF)
+
+        write(g, 0, om, mixed)
+
+    def grad_out(g):
+        wait_bytes(gh.at[g], bk_r.at[g])
+
+        @pl.loop(0, 4)
+        def _(i):
+            js = pl.ds(i * 4, 4)
+            rows = pl.ds(pl.multiple_of(g * 256 + c * 128 + i * 32, 32), 32)
+            gh[g, js] = (gh[g, js].astype(F32) + cotm[rows, :].astype(F32).reshape(4, 8, 2048)).astype(BF)
+
+        write(g, 1, gh, grad)
 
     def w_terms(i):
         @pl.loop(0, 8)
@@ -367,7 +430,7 @@
         @pl.loop(0, 2)
         def _(b):
             cols = pl.ds(pl.multiple_of(b * 256, 256), 256)
-            wo[pl.ds(2 * b, 2)] = tn(back[3, :, cols], cotm[...]).reshape(2, 4, 4, 8, 2048).astype(BF)
+            wo[pl.ds(2 * b, 2)] = tn(attm[:, cols], cotm[...]).reshape(2, 4, 4, 8, 2048).astype(BF)
 
     rs = (rs_s, rs_r)
 
@@ -423,15 +486,22 @@
     cols_i = lax.broadcasted_iota(jnp.int32, (128, 128), 1)
     same = lax.rem(rows_i + 128 - cols_i, 8) == 0
     mask[...] = jnp.where(same & (cols_i <= rows_i), 0.0, -1e30)
-    for a, b in zip(firsts, seconds):
+    for a, b in ((da, db), (ea, eb), (fa, fb), (qa, qb), (ka, kb), (va, vb)):
         a.arrive()
         b.start()
-    for a, b in zip(seconds, thirds):
+    for a, b in ((db, dc), (eb, ec), (fb, fc), (qb, qc), (kb, kc), (vb, vc)):
         a.arrive()
         b.start()
     spread(0)
-    for r in thirds:
+    cot_rows()
+    for r in (dc, ec, fc):
         r.relay()
+    for r in (qc, kc, vc):
+        r.relay()
+    for r in (dc, ec, fc):
+        r.arrive()
+    wo_rows()
+    upstream()
     spread(1)
     pass_on(0)
     norm(0)
@@ -439,68 +509,75 @@
     project(0, 0)
     vc.arrive()
     project(0, 2)
-    spread(2)
-    for r in (dc, ec, fc):
-        r.arrive()
-
-    @pl.loop(0, 4)
-    def _(j):
-        wom[pl.ds(pl.multiple_of(j * 128, 128), 128), :] = wo[j].astype(F32).reshape(128, 2048).astype(BF)
-
-    project(0, 3)
     kc.arrive()
     project(0, 1)
+    spread(2)
+    wait_bytes(upt, up_r.at[0])
+    project(0, 3)
     attention(0)
+    partials(0)
     pass_on(1)
-    partials(0)
     norm(1)
     for i in range(4):
         project(1, i)
+    pass_on(2)
     finalize(0)
     attention(1)
-    pass_on(2)
     partials(1)
     norm(2)
     for i in range(4):
         project(2, i)
     finalize(1)
     attention(2)
+    for r in rings:
+        r.finish()
+    for copy in swap_c:
+        copy.wait_send()
     partials(2)
+    w_terms(0)
+    qx.start()
+    home_rows(0)
+    home_rows(1)
+    w_terms(1)
+    kx.start()
+    home_rows(2)
+    o_terms()
+    for r in (dx, ex, fx):
+        r.start()
+    w_terms(2)
+    vx.start()
+    finalize(2)
+    qx.relay()
+    kx.relay()
+    for r in (dx, ex, fx):
+        r.relay()
+    home(0)
+    vx.relay()
     for i in range(16):
         gland[9, pl.ds(i, 1), :] = gg[:, pl.ds(128 * i, 128)]
     g0 = gain_start(0, gland.at[9])
-    for r in rings:
-        r.finish()
-    o_terms()
-    for r in (dx, ex, fx):
-        r.start()
-    w_terms(0)
-    qx.start()
-    w_terms(1)
-    kx.start()
-    finalize(2)
-    w_terms(2)
-    vx.start()
-    for r in (dx, ex, fx):
-        r.relay()
-    qx.relay()
-    kx.relay()
+    home(1)
+    home(2)
+    for a, b in ((qx, qy), (kx, ky), (dx, dy), (ex, ey), (fx, fy)):
+        a.finish()
+        b.start()
     gain_finish(0, gland.at[9], g0)
     g1 = gain_start(1, gacc.at[0])
-    vx.relay()
-    for a, b in ((dx, dy), (ex, ey), (fx, fy)):
-        a.finish()
-        b.start()
-    for a, b in ((qx, qy), (kx, ky)):
+    vx.finish()
+    vy.start()
+    mixed_out(0)
+    mixed_out(1)
+    mixed_out(2)
+    grad_out(0)
+    grad_out(1)
+    for a, b in ((qy, qz), (ky, kz), (dy, dz), (ey, ez), (fy, fz)):
         a.finish()
         b.start()
     gain_finish(1, gacc.at[0], g1)
     g2 = gain_start(2, gacc.at[1])
-    vx.finish()
-    vy.start()
-    for a, b in ((dy, dz), (ey, ez), (fy, fz), (qy, qz), (ky, kz), (vy, vz)):
-        a.finish()
-        b.start()
+    vy.finish()
+    vz.start()
+    grad_out(2)
     gain_finish(2, gacc.at[1], g2)
     g3 = rcopy(gacc.at[2], gland.at[10], (gn_s, gn_r), 9, sib)
     g3.start()
@@ -529,10 +606,13 @@
     put(0, g_q)
     put(1, g_k)
     put(2, g_v)
-    for j, (src, dst) in enumerate([(om, mixed), (og, grad)]):
-        wait_bytes(dst, bk_r.at[j])
-        wait_bytes(src.at[:, pl.ds(0, 15)], bk_s.at[j])
-    for copies in (swap_w, passed[0], passed[1], passed[2], swapped[0], swapped[1], swapped[2], g0, g1, g2, [g3], list(last.values())):
+    wait_bytes(ups.at[:, :, pl.ds(0, 15)], up_s.at[0])
+    for g in range(3):
+        wait_bytes(atts.at[g, :, pl.ds(0, 15)], at_s.at[g])
+        wait_bytes(og.at[g, pl.ds(0, 15)], bk_s.at[g])
+    for copy in written:
+        copy.wait()
+    for copies in (swap_w, passed.values(), swapped.values(), mixed_swap.values(), g0, g1, g2, [g3], last.values()):
         for copy in copies:
             copy.wait_send()
     for r in all_sums:
@@ -554,7 +634,7 @@
     def out_sums(n):
         return ring((), (2, 4, 8, n)) + [V(u, BF) for u in ((4, 4, 8, n), (3, 4, 8, n), (4, 8, n), (3, 1, 8, n))]
 
-    sems = [60, 60, 12, 12, 12, 6, 6, 6, 6, 9, 9, 2, 2, 72, 72, 10, 10, 7]
+    sems = [60, 60, 12, 12, 12, 3, 3, 3, 3, 3, 3, 1, 1, 3, 3, 9, 9, 3, 3, 72, 72, 10, 10, 7, 6]
     return pl.pallas_call(
         block_kernel,
         out_shape=(sds(rows, BF), sds(rows, BF))
@@ -562,11 +642,15 @@
         + (sds((8, 2048), F32), sds((16, 128), F32)),
         in_specs=[any_] * 6 + [vm],
         out_specs=(any_, any_) + (vm,) * 5,
-        scratch_shapes=[V((2, 3, 16, 8, 2048), BF)] * 2
+        scratch_shapes=[V((2, 3, 16, 8, 2048), BF), V((3, 2, 16, 8, 2048), BF)]
         + [V((3, 4, 2, 4, 4, 16, 512), BF), V((4, 4, 4, 8, 2048), BF), V((512, 2048), BF)]
         + [V((768, 2048), BF)] * 2
-        + [V((256, 2048), F32), V((4, 256, 512), BF), V((4, 768, 512), BF), V((128, 128), F32)]
-        + [V((3, 2, 16, 8, 2048), BF)] * 2
+        + [V((256, 2048), F32), V((4, 256, 512), BF)]
+        + [V((3, 2, 16, 8, 512), BF)] * 2
+        + [V((3, 768, 512), BF)]
+        + [V((3, 2, 16, 8, 512), BF)] * 2
+        + [V((768, 512), BF), V((128, 128), F32)]
+        + [V(groups, BF), V((3, 2, 16, 8, 2048), BF)]
         + [V(groups, BF)] * 4
         + ring((3,), (4, 4, 16, 512))
         + [V((3, 2, 4, 4, 16, 512), BF)]

time: 170 us -> 156 us (0.918)
  Pallas kernels: 167 us -> 154 us
    pallas_call x1, Pallas kernels: 163 us -> 150 us  [block_call(): pl.pallas_call(block_kernel, out_shape=(sds(rows, BF), sds(rows, BF)) + (...]
where the time goes in v4:
time: 156 us
  Pallas kernels  154 us (99%)
    pallas_call x1, Pallas kernels, block_call(): pl.pallas_call(block_kernel, out_shape=(sds(rows, BF), sds(rows, BF)) + (...  150 us
    pallas_call x1, Pallas kernels, finish_call(): pl.pallas_call(finish_kernel, out_shape=tuple((jax.ShapeDtypeStruct(a.sha...  4.15 us

profile of v4, /device:TPU:1, one launch (start us, length us, event | category | flops | bytes accessed | tf_op | source)
XLA Modules:
  0.0 156.1 jit_solution(9863437747139092372)
XLA Ops:
  0.6 1.3 reshape.34.gain
  1.9 149.8 %block.1 = (bf16[16,3,8,2048]{3,2,1,0:T(8,128)(2,1)}, bf16[16,3,8,2048]{3,2,1,0:T(8,128)(2,1)}, f32[16,1024]{1,0:T(8,128)}, f32[16,1024]{1,0:T(8,128)}, f32[16,1...) custom-call(bf16[16,3,8,2048]{3,2,1,0:T(8,128)(2,1)} %bitcast.5, bf16[16,3,8,2048]{3,2,1,0:T(8,128)(2,1)} %bitcast.6, ...), custom_call_target="tpu_custom_call" | custom-call | tf_op jit(solution)/shard_map/block/pallas_call | solution.py:638
  151.8 4.1 %finish.1 = (bf16[16,3,8,2048]{3,2,1,0:T(8,128)(2,1)}, bf16[16,3,8,2048]{3,2,1,0:T(8,128)(2,1)}, f32[16,1024]{1,0:T(8,128)}, f32[16,1024]{1,0:T(8,128)}, f32[16,...) custom-call(bf16[16,3,8,2048]{3,2,1,0:T(8,128)(2,1)} %get-tuple-element.21.refs_0_, ...), custom_call_target="tpu_custom_call" | custom-call | tf_op jit(solution)/shard_map/finish/pallas_call | solution.py:695

commit v5 on v4

--- a/solution.py
+++ b/solution.py
@@ -187,13 +187,13 @@
     pltpu.make_async_copy(ref, ref, sem).wait()
 
 
-def block_kernel(tok, cot, wq, wk, wv, w_out, gain, mixed, grad, g_q, g_k, g_v, g_o, gsum,
+def block_kernel(tok, cot, wq, wk, wv, w_out, gain_in, mixed, grad, g_q, g_k, g_v, g_o, gsum,
                  t, cth, w, wo, wom, normed, cotm, scaled, proj, ups, upt, back, atts, atth, attm, mask,
                  mrh, dp, dr, om, og, gh,
                  via1, land1, sum1, land2, sum2, land3, p3, p3r,
                  dvia, dland, d1, dland2, d2, dland3, evia, eland, e1, eland2, e2, eland3,
                  fvia, fland, f1, fland2, f2, fland3, q3,
-                 gg, gland, gacc,
+                 gain, gg, gland, gacc,
                  ag_s, ag_r, w_s, w_r, w_l, in_s, in_r, fw_s, fw_r, c_s, c_r, up_s, up_r, at_s, at_r, sw_s, sw_r,
                  bk_s, bk_r, rs_s, rs_r, gn_s, gn_r, loc, out_l):
     y, c, z, x = coords()
@@ -314,7 +314,7 @@
             s = centered * inverse
             scaled[pl.ds(pl.multiple_of(i * 32, 32), 32), :] = s
             rows = pl.ds(pl.multiple_of(g * 256 + i * 32, 32), 32)
-            normed[rows, :] = (s * gain[...].astype(F32)).astype(BF)
+            normed[rows, :] = (s * gain[...]).astype(BF)
 
     def project(g, i):
         rows = pl.ds(g * 256, 256)
@@ -371,7 +371,7 @@
             centered = value - jnp.mean(value, axis=-1, keepdims=True)
             inverse = lax.rsqrt(jnp.mean(centered * centered, axis=-1, keepdims=True) + 1e-05)
             s = centered * inverse
-            ds = (dp[g, c, fs].astype(F32) + dr[g, fs].astype(F32)) * gain[...].astype(F32).reshape(1, 1, 2048)
+            ds = (dp[g, c, fs].astype(F32) + dr[g, fs].astype(F32)) * gain[...].reshape(1, 1, 2048)
             first = jnp.mean(ds, axis=-1, keepdims=True)
             second = jnp.mean(ds * s, axis=-1, keepdims=True)
             og[g, fs] = (inverse * (ds - first - s * second)).astype(BF)
@@ -482,6 +482,7 @@
         copy.wait_recv()
     for r in (qa, ka, va):
         r.start()
+    gain[...] = gain_in[...].astype(F32).reshape(1, 2048)
     rows_i = lax.broadcasted_iota(jnp.int32, (128, 128), 0)
     cols_i = lax.broadcasted_iota(jnp.int32, (128, 128), 1)
     same = lax.rem(rows_i + 128 - cols_i, 8) == 0
@@ -662,7 +663,7 @@
         + out_sums((2048 - CUT) // 2)
         + out_sums((2048 - CUT) // 2)
         + [V((1, 8, 2048), F32)]
-        + [V((1, 2048), F32), V((11, 16, 128), F32), V((3, 16, 128), F32)]
+        + [V((1, 2048), F32), V((1, 2048), F32), V((11, 16, 128), F32), V((3, 16, 128), F32)]
         + [sem((n,)) for n in sems],
         compiler_params=pltpu.CompilerParams(collective_id=0, has_side_effects=True, vmem_limit_bytes=VMEM_LIMIT),
         name="block",
@@ -705,7 +706,7 @@
 def on_device(tokens, cotangent, norm_gain, w_query, w_key, w_value, w_out):
     tok = tokens.reshape(16, 3, 8, 2048)
     cot = cotangent.reshape(16, 3, 8, 2048)
-    gain = norm_gain.reshape(1, 2048)
+    gain = norm_gain
     *arrays, gsum = block_call(tok, cot, w_query, w_key, w_value, w_out, gain)
     mixed, grad, g_q, g_k, g_v, g_o, grad_gain = finish_call(arrays, gsum)
     shape = (1, 1, 384, 2048)

time: 156 us -> 155 us (level)
  no operation moved by 1% of the time
where the time goes in v5:
time: 155 us
  Pallas kernels  154 us (99%)
    pallas_call x1, Pallas kernels, block_call(): pl.pallas_call(block_kernel, out_shape=(sds(rows, BF), sds(rows, BF)) + (...  150 us
    pallas_call x1, Pallas kernels, finish_call(): pl.pallas_call(finish_kernel, out_shape=tuple((jax.ShapeDtypeStruct(a.sha...  4.15 us

profile of v5, /device:TPU:1, one launch (start us, length us, event | category | flops | bytes accessed | tf_op | source)
XLA Modules:
  0.0 154.9 jit_solution(3271731645559088033)
XLA Ops:
  0.6 149.9 %block.1 = (bf16[16,3,8,2048]{3,2,1,0:T(8,128)(2,1)}, bf16[16,3,8,2048]{3,2,1,0:T(8,128)(2,1)}, f32[16,1024]{1,0:T(8,128)}, f32[16,1024]{1,0:T(8,128)}, f32[16,1...) custom-call(bf16[16,3,8,2048]{3,2,1,0:T(8,128)(2,1)} %bitcast.5, bf16[16,3,8,2048]{3,2,1,0:T(8,128)(2,1)} %bitcast.6, ...), custom_call_target="tpu_custom_call" | custom-call | tf_op jit(solution)/shard_map/block/pallas_call | solution.py:639
  150.6 4.1 %finish.1 = (bf16[16,3,8,2048]{3,2,1,0:T(8,128)(2,1)}, bf16[16,3,8,2048]{3,2,1,0:T(8,128)(2,1)}, f32[16,1024]{1,0:T(8,128)}, f32[16,1024]{1,0:T(8,128)}, f32[16,...) custom-call(bf16[16,3,8,2048]{3,2,1,0:T(8,128)(2,1)} %get-tuple-element.21.refs_0_, ...), custom_call_target="tpu_custom_call" | custom-call | tf_op jit(solution)/shard_map/finish/pallas_call | solution.py:696

commit v6 on v5

--- a/solution.py
+++ b/solution.py
@@ -8,7 +8,7 @@
 from jax.sharding import PartitionSpec as P
 
 MESH = pl.DeviceIdType.MESH
-CUT = 1024
+CUT = 768
 VMEM_LIMIT = 62 * 1024 * 1024
 
 

time: 155 us -> 157 us (1.013)
  Pallas kernels: 154 us -> 156 us
    pallas_call x1, Pallas kernels: 150 us -> 152 us  [block_call(): pl.pallas_call(block_kernel, out_shape=(sds(rows, BF), sds(rows, BF)) + (...]
where the time goes in v6:
time: 157 us
  Pallas kernels  156 us (99%)
    pallas_call x1, Pallas kernels, block_call(): pl.pallas_call(block_kernel, out_shape=(sds(rows, BF), sds(rows, BF)) + (...  152 us
    pallas_call x1, Pallas kernels, finish_call(): pl.pallas_call(finish_kernel, out_shape=tuple((jax.ShapeDtypeStruct(a.sha...  4.15 us

profile of v6, /device:TPU:1, one launch (start us, length us, event | category | flops | bytes accessed | tf_op | source)
XLA Modules:
  0.0 156.9 jit_solution(4166322987160870836)
XLA Ops:
  0.6 151.9 %block.1 = (bf16[16,3,8,2048]{3,2,1,0:T(8,128)(2,1)}, bf16[16,3,8,2048]{3,2,1,0:T(8,128)(2,1)}, f32[16,1024]{1,0:T(8,128)}, f32[16,1024]{1,0:T(8,128)}, f32[16,1...) custom-call(bf16[16,3,8,2048]{3,2,1,0:T(8,128)(2,1)} %bitcast.5, bf16[16,3,8,2048]{3,2,1,0:T(8,128)(2,1)} %bitcast.6, ...), custom_call_target="tpu_custom_call" | custom-call | tf_op jit(solution)/shard_map/block/pallas_call | solution.py:639
  152.6 4.1 %finish.1 = (bf16[16,3,8,2048]{3,2,1,0:T(8,128)(2,1)}, bf16[16,3,8,2048]{3,2,1,0:T(8,128)(2,1)}, f32[16,1024]{1,0:T(8,128)}, f32[16,1024]{1,0:T(8,128)}, f32[16,...) custom-call(bf16[16,3,8,2048]{3,2,1,0:T(8,128)(2,1)} %get-tuple-element.21.refs_0_, ...), custom_call_target="tpu_custom_call" | custom-call | tf_op jit(solution)/shard_map/finish/pallas_call | solution.py:696
